TPU v7x, 512 devices: a whole 4x8x8 slice. The times are simulated.
512 devices in a mesh: head: 4 (over z_lo, core), inner: 8 (over y), outer: 16 (over z_hi, x).
Axes of the slice: x: 4, y: 8, z: 8 (z_hi: 4, z_lo: 2; z = z_hi * 2 + z_lo), core: 2. Of those that a mesh axis runs over, the one named last changes fastest.
Arguments:
- queries: bfloat16 [16384, 6144], P(('outer', 'inner', 'head')), may hold values from -6 to 6
- keys: bfloat16 [16384, 1024], P(('outer', 'inner', 'head')), may hold values from -6 to 6
- values: bfloat16 [16384, 1024], P(('outer', 'inner', 'head')), may hold values from -6 to 6
- grad_out: bfloat16 [16384, 6144], P(('outer', 'inner', 'head')), may hold values from -6 to 6
- positions: int32 [16384], P(('outer', 'inner')), may hold values from 0 to 16383, as said below
Outputs:
- grad_queries: bfloat16 [16384, 6144], P(('outer', 'inner', 'head'))
- grad_keys: bfloat16 [16384, 1024], P(('outer', 'inner', 'head'))
- grad_values: bfloat16 [16384, 1024], P(('outer', 'inner', 'head'))
Inputs may be any that keep to these rules, and one draw needn't show every extreme that they name: Rows o * 1024 to (o + 1) * 1024 - 1 hold a permutation of the positions o * 1024 to (o + 1) * 1024 - 1, in aligned runs of 64 rows whose positions are consecutive and increasing.
All inputs are finite; a program needn't handle non-finite values.
Results may differ from a plain program's by a relative error of at most 0.019.
Values may be sent and summed in bfloat16 or wider, within the bound.
A program may use at most 64 MiB of HBM per device.

v0:
```python
import jax
import jax.numpy as jnp
from jax import lax
from jax.sharding import PartitionSpec as P

D_HEAD = 128


def passed_along(value, axis, by):
    peers = lax.axis_size(axis)
    return lax.ppermute(value, axis, [(i, (i + by) % peers) for i in range(peers)])


def passed_along_2(value, axis, steps):
    count = lax.axis_size(axis)
    initial, last = (max(0, -steps), min(count, count - steps))
    return lax.ppermute(value, axis, [(source, source + steps) for source in range(initial, last)])


def attend(query_rows, upstream_rows, query_pos, key_all, value_all, key_pos, block_len, kv_heads):
    row_count = query_rows.shape[0]
    softmax_scale = D_HEAD ** (-0.5)
    query = query_rows.reshape(row_count, kv_heads, -1, D_HEAD)
    upstream = upstream_rows.reshape(row_count, kv_heads, -1, D_HEAD)
    per_group = query.shape[2]
    total_keys = key_all.shape[0]
    block_count = total_keys // 512
    block_width = total_keys // block_count
    key_blocks = key_all.reshape(block_count, block_width, kv_heads, D_HEAD)
    value_blocks = value_all.reshape(block_count, block_width, kv_heads, D_HEAD)
    pos_blocks = key_pos.reshape(block_count, block_width)
    query_block = query_pos // block_len

    def scored(key_blk, pos_blk):
        logits = (
            jnp.einsum("qhgd,khd->hgqk", query, key_blk, preferred_element_type=jnp.float32)
            * softmax_scale
        )
        allowed = (pos_blk[None, :] <= query_pos[:, None]) & (
            query_block[:, None] - pos_blk[None, :] // block_len <= 1
        )
        return (logits, allowed)

    def statistics(carry, piece):
        highest, summed = carry
        logits, allowed = scored(piece[0], piece[1])
        masked = jnp.where(allowed, logits, -jnp.inf)
        new_high = jnp.maximum(highest, jnp.max(masked, axis=-1))
        summed = summed * jnp.exp(highest - new_high) + jnp.sum(
            jnp.exp(masked - new_high[..., None]), axis=-1
        )
        return ((new_high, summed), None)

    stat_shape = (kv_heads, per_group, row_count)
    start_stats = (jnp.full(stat_shape, -1e30, jnp.float32), jnp.zeros(stat_shape, jnp.float32))
    (highest, summed), _ = lax.scan(statistics, start_stats, (key_blocks, pos_blocks))
    lse = highest + jnp.log(summed)

    def weights(key_blk, pos_blk):
        logits, allowed = scored(key_blk, pos_blk)
        return jnp.where(allowed, jnp.exp(logits - lse[..., None]), 0.0)

    def forward(running, piece):
        probs_half = weights(piece[0], piece[2]).astype(jnp.bfloat16)
        running = running + jnp.einsum(
            "hgqk,khd->hgqd", probs_half, piece[1], preferred_element_type=jnp.float32
        )
        return (running, None)

    attended, _ = lax.scan(
        forward,
        jnp.zeros((kv_heads, per_group, row_count, D_HEAD), jnp.float32),
        (key_blocks, value_blocks, pos_blocks),
    )
    row_delta = jnp.sum(
        attended * jnp.transpose(upstream, (1, 2, 0, 3)).astype(jnp.float32), axis=-1
    )

    def backward(running, piece):
        key_blk, value_blk, pos_blk = piece
        probs = weights(key_blk, pos_blk)
        dprobs = jnp.einsum(
            "qhgd,khd->hgqk", upstream, value_blk, preferred_element_type=jnp.float32
        )
        dscores = (probs * (dprobs - row_delta[..., None])).astype(jnp.bfloat16)
        probs_half = probs.astype(jnp.bfloat16)
        running = running + jnp.einsum(
            "hgqk,khd->qhgd", dscores, key_blk, preferred_element_type=jnp.float32
        )
        key_term = (
            jnp.einsum("hgqk,qhgd->khd", dscores, query, preferred_element_type=jnp.float32)
            * softmax_scale
        )
        value_term = jnp.einsum(
            "hgqk,qhgd->khd", probs_half, upstream, preferred_element_type=jnp.float32
        )
        return (running, (key_term, value_term))

    start_grad = jnp.zeros((row_count, kv_heads, per_group, D_HEAD), jnp.float32)
    grad_query, (key_terms, value_terms) = lax.scan(
        backward, start_grad, (key_blocks, value_blocks, pos_blocks)
    )
    grad_query = (grad_query * softmax_scale).astype(jnp.bfloat16).reshape(row_count, -1)
    key_terms = key_terms.reshape(total_keys, kv_heads * D_HEAD)
    value_terms = value_terms.reshape(total_keys, kv_heads * D_HEAD)
    return (grad_query, key_terms, value_terms)


def on_device(queries, keys, values, grad_out, positions):
    query_rows, key_rows, value_rows, upstream_rows = (
        lax.all_to_all(queries, "head", split_axis=1, concat_axis=0, tiled=True),
        lax.all_to_all(keys, "head", split_axis=1, concat_axis=0, tiled=True),
        lax.all_to_all(values, "head", split_axis=1, concat_axis=0, tiled=True),
        lax.all_to_all(grad_out, "head", split_axis=1, concat_axis=0, tiled=True),
    )
    row_count = query_rows.shape[0]
    kv_width = key_rows.shape[1]
    kv_heads = kv_width // D_HEAD
    block_len = row_count * lax.axis_size("inner")
    own_keys, own_values, own_pos = (
        lax.all_gather(key_rows, "inner", axis=0, tiled=True),
        lax.all_gather(value_rows, "inner", axis=0, tiled=True),
        lax.all_gather(positions, "inner", axis=0, tiled=True),
    )
    prior_keys, prior_values, prior_pos = passed_along((own_keys, own_values, own_pos), "outer", 1)
    key_all = jnp.concatenate([own_keys, prior_keys], axis=0)
    value_all = jnp.concatenate([own_values, prior_values], axis=0)
    key_pos = jnp.concatenate([own_pos, prior_pos], axis=0)
    grad_query, key_terms, value_terms = attend(
        query_rows, upstream_rows, positions, key_all, value_all, key_pos, block_len, kv_heads
    )
    half_keys = key_terms.shape[0] // 2
    back_keys, back_values = (
        passed_along_2(key_terms[half_keys:].astype(jnp.bfloat16), "outer", -1).astype(jnp.float32),
        passed_along_2(value_terms[half_keys:].astype(jnp.bfloat16), "outer", -1).astype(
            jnp.float32
        ),
    )
    summed_keys = key_terms[:half_keys] + back_keys
    summed_values = value_terms[:half_keys] + back_values
    combined = lax.psum_scatter(
        jnp.concatenate([summed_keys, summed_values], axis=1).astype(jnp.bfloat16),
        "inner",
        scatter_dimension=0,
        tiled=True,
    ).astype(jnp.float32)
    grad_key = combined[:, :kv_width].astype(jnp.bfloat16)
    grad_value = combined[:, kv_width:].astype(jnp.bfloat16)
    return (
        lax.all_to_all(grad_query, "head", split_axis=0, concat_axis=1, tiled=True),
        lax.all_to_all(grad_key, "head", split_axis=0, concat_axis=1, tiled=True),
        lax.all_to_all(grad_value, "head", split_axis=0, concat_axis=1, tiled=True),
    )


def solution(mesh):
    return jax.shard_map(
        on_device,
        mesh=mesh,
        in_specs=(
            P(("outer", "inner", "head"), None),
            P(("outer", "inner", "head"), None),
            P(("outer", "inner", "head"), None),
            P(("outer", "inner", "head"), None),
            P(("outer", "inner")),
        ),
        out_specs=(
            P(("outer", "inner", "head"), None),
            P(("outer", "inner", "head"), None),
            P(("outer", "inner", "head"), None),
        ),
        check_vma=False,
    )
```

profile of v0, /device:TPU:7, one launch (start us, length us, event | category | flops | bytes accessed | tf_op | source)
XLA Modules:
  0.0 319.7 jit_solution(2793065654841149436)
XLA Ops:
  8.6 4.3 %all-to-all-start = ((bf16[32,4,256]{2,0,1:T(8,128)(2,1)}), bf16[32,4,256]{2,0,1:T(8,128)(2,1)S(1)}, u32[]{:S(2)}, u32[]{:S(2)}) async-start(bf16[32,4,256]{2,0,1:T(8,128)(2,1)} %bitcast.182), calls=%async_computation | async-start | bytes 131072 | tf_op jit(solution)/shard_map/all_to_all | solution.py:112
  14.4 1.8 all-to-all-done
  16.2 4.1 %all-to-all-start.2 = ((bf16[32,4,256]{2,0,1:T(8,128)(2,1)}), bf16[32,4,256]{2,0,1:T(8,128)(2,1)S(1)}, u32[]{:S(2)}, u32[]{:S(2)}) async-start(bf16[32,4,256]{2,0,1:T(8,128)(2,1)} %bitcast.181), calls=%async_computation.2 | async-start | bytes 131072 | tf_op jit(solution)/shard_map/all_to_all | solution.py:113
  20.3 1.8 copy.116
  23.6 4.3 %all-to-all-start.1 = ((bf16[32,4,1536]{2,0,1:T(8,128)(2,1)}), bf16[32,4,1536]{2,0,1:T(8,128)(2,1)S(1)}, u32[]{:S(2)}, u32[]{:S(2)}) async-start(bf16[32,4,1536]{2,0,1:T(8,128)(2,1)} %bitcast.180), calls=%async_computation.1 | async-start | bytes 786432 | tf_op jit(solution)/shard_map/all_to_all | solution.py:111
  27.9 13.0 %all-gather = s32[8,1,128]{2,1,0:T(1,128)S(1)} all-gather(s32[1,1,128]{2,1,0:T(1,128)} %bitcast.2), channel_id=1, replica_groups=mesh['head'=4,'inner'=8,'outer'=16] {'inner'}, dimensions={0}, use_global_device_ids=true | all-gather | bytes 4608 | tf_op jit(solution)/shard_map/all_gather | solution.py:123
  40.9 5.7 %collective-permute-start.1 = (s32[1024]{0:T(1024)S(1)}, s32[1024]{0:T(1024)S(1)}, u32[]{:S(2)}, u32[]{:S(2)}) collective-permute-start(s32[1024]{0:T(1024)S(1)} %bitcast.270), channel_id=1, source_target_pairs={{0,1},{1,2},{2,3},{3,4},{4,5},{5,6},{6,7},{7,8},{8,9},{9,10},{10,1... | collective-permute-start | bytes 12296 | tf_op jit(solution)/shard_map/ppermute | solution.py:11
  46.6 1.8 copy.115
  48.4 7.5 %all-to-all-start.3 = ((bf16[32,4,1536]{2,0,1:T(8,128)(2,1)}), bf16[32,4,1536]{2,0,1:T(8,128)(2,1)S(1)}, u32[]{:S(2)}, u32[]{:S(2)}) async-start(bf16[32,4,1536]{2,0,1:T(8,128)(2,1)} %bitcast.179), calls=%async_computation.3 | async-start | bytes 786432 | tf_op jit(solution)/shard_map/all_to_all | solution.py:114
  56.0 19.8 %all_gather.9 = bf16[1024,256]{1,0:T(8,128)(2,1)S(1)} all-gather(bf16[128,256]{1,0:T(8,128)(2,1)S(1)} %bitcast.256), channel_id=1, replica_groups=mesh['head'=4,'inner'=8,'outer'=16] {'inner'}, dimensions={0}, use_global_device_ids=true | all-gather | bytes 589824 | tf_op jit(solution)/shard_map/all_gather | solution.py:121
  75.8 3.1 collective-permute-start
  81.9 21.3 %all_gather.11 = bf16[1024,256]{1,0:T(8,128)(2,1)} all-gather(bf16[128,256]{1,0:T(8,128)(2,1)S(1)} %bitcast.255), channel_id=1, replica_groups=mesh['head'=4,'inner'=8,'outer'=16] {'inner'}, dimensions={0}, use_global_device_ids=true | all-gather | bytes 589824 | tf_op jit(solution)/shard_map/all_gather | solution.py:122
  103.2 3.3 %collective-permute-start.2 = (bf16[1024,256]{1,0:T(8,128)(2,1)}, bf16[1024,256]{1,0:T(8,128)(2,1)}, u32[]{:S(2)}, u32[]{:S(2)}) collective-permute-start(bf16[1024,256]{1,0:T(8,128)(2,1)} %all_gather.11), channel_id=1, source_target_pairs={{0,1},{1,2},{2,3},{3,4},{4,5},{5,6},{6,7},{7,8},{8,9},{9,10},{10,1... | collective-permute-start | bytes 1572872 | tf_op jit(solution)/shard_map/ppermute | solution.py:11
  109.9 23.6 %while.45 = (s32[]{:T(128)}, f32[2,6,128]{2,1,0:T(8,128)S(1)}, f32[2,6,128]{2,1,0:T(8,128)}, s32[4,512]{1,0:T(4,128)}, s32[128]{0:T(128)}, /*index=5*/s32[128]{0...) while((s32[]{:T(128)}, f32[2,6,128]{2,1,0:T(8,128)S(1)}, ...), condition=%wide.region_3.4_spmd.clone, body=%wide.region_0.3_spmd.clone.sunk | while | flops 207109120 | bytes 7546568 | solution.py:56
  112.1 1.5 fusion.93
  118.0 1.5 fusion.93
  123.9 1.5 fusion.93
  129.8 1.5 fusion.93
  136.3 16.5 %while.46 = (s32[]{:T(128)}, f32[2,6,128,128]{3,2,1,0:T(8,128)S(1)}, s32[4,512]{1,0:T(4,128)}, s32[128]{0:T(128)}, s32[128]{0:T(128)}, /*index=5*/bf16[4,512,2,1...) while((s32[]{:T(128)}, ...), condition=%wide.region_5.6_spmd.clone, body=%wide.region_4.5_spmd.clone.sunk | while | flops 406461952 | bytes 2639995 | solution.py:70
  138.0 2.5 fusion.99
  142.1 2.5 fusion.99
  146.3 2.5 fusion.99
  150.4 2.5 fusion.99
  153.7 46.7 %while.47 = (s32[]{:T(128)}, f32[128,2,6,128]{0,3,2,1:T(8,128)S(1)}, f32[4,512,2,128]{3,1,2,0:T(8,128)}, f32[4,512,2,128]{3,1,2,0:T(8,128)}, bf16[4,512,2,128]{3...) while((s32[]{:T(128)}, ...), condition=%wide.region_8.9_spmd.clone, body=%wide.region_7.8_spmd.clone.sunk | while | flops 1015291392 | bytes 46104304 | solution.py:100
  155.3 1.5 fusion.110
  156.9 1.7 copy-done
  158.6 2.0 fusion.112
  162.0 1.6 fusion.113
  167.0 1.5 fusion.110
  168.6 1.7 copy-done
  170.3 2.0 fusion.112
  173.6 1.6 fusion.113
  180.2 1.7 copy-done
  181.9 2.0 fusion.112
  185.3 1.6 fusion.113
  190.4 1.5 fusion.110
  191.9 1.7 copy-done
  193.6 2.0 fusion.112
  197.0 1.6 fusion.113
  202.5 2.2 collective-permute-start.3
  205.4 2.2 collective-permute-start.4
  210.6 30.5 %collective-permute-done.3 = bf16[1024,256]{1,0:T(8,128)(2,1)S(1)} collective-permute-done((bf16[1024,256]{1,0:T(8,128)(2,1)S(1)}, bf16[1024,256]{1,0:T(8,128)(2,1)S(1)}, u32[]{:S(2)}, u32[]{:S(2)}) %collective-permute-start.3) | collective-permute-done | bytes 524320 | tf_op jit(solution)/shard_map/ppermute | solution.py:17
  241.2 11.1 %collective-permute-done.4 = bf16[1024,256]{1,0:T(8,128)(2,1)S(1)} collective-permute-done((bf16[1024,256]{1,0:T(8,128)(2,1)S(1)}, bf16[1024,256]{1,0:T(8,128)(2,1)S(1)}, u32[]{:S(2)}, u32[]{:S(2)}) %collective-permute-start.4) | collective-permute-done | bytes 524320 | tf_op jit(solution)/shard_map/ppermute | solution.py:17
  255.3 6.6 %all-to-all-start.4 = ((bf16[4,32,1536]{2,1,0:T(8,128)(2,1)}), bf16[4,32,1536]{2,1,0:T(8,128)(2,1)S(1)}, u32[]{:S(2)}, u32[]{:S(2)}) async-start(bf16[4,32,1536]{2,1,0:T(8,128)(2,1)} %all_to_all.108), calls=%async_computation.4 | async-start | bytes 786432 | tf_op jit(solution)/shard_map/all_to_all | solution.py:150
  261.9 29.8 %reduce-scatter.2.cloned.1.call-done = bf16[128,512]{1,0:T(8,128)(2,1)} async-done(((bf16[1024,512]{1,0:T(8,128)(2,1)}), bf16[128,512]{1,0:T(8,128)(2,1)}) %reduce-scatter.2.cloned.1.call-update) | async-done | bytes 131088 | tf_op jit(solution)/shard_map/reduce_scatter | solution.py:141
  293.3 11.6 %all_to_all.127 = bf16[4,32,256]{2,1,0:T(8,128)(2,1)S(1)} all-to-all(bf16[4,32,256]{2,1,0:T(8,128)(2,1)S(1)} %bitcast.259), channel_id=1, replica_groups=mesh['head'=4,'inner'=8,'outer'=16] {'head'}, dimensions={0} | all-to-all | bytes 131072 | tf_op jit(solution)/shard_map/all_to_all | solution.py:151
  304.9 4.1 %all-to-all-start.6 = ((bf16[4,32,256]{2,1,0:T(8,128)(2,1)}), bf16[4,32,256]{2,1,0:T(8,128)(2,1)S(1)}, u32[]{:S(2)}, u32[]{:S(2)}) async-start(bf16[4,32,256]{2,1,0:T(8,128)(2,1)} %bitcast.12), calls=%async_computation.7 | async-start | bytes 131072 | tf_op jit(solution)/shard_map/all_to_all | solution.py:152
  310.4 1.9 all-to-all-done.6
  (161 shorter events, 71.1 us)
Async XLA Ops:
  8.6 7.6 %all-to-all-start = ((bf16[32,4,256]{2,0,1:T(8,128)(2,1)}), bf16[32,4,256]{2,0,1:T(8,128)(2,1)S(1)}, u32[]{:S(2)}, u32[]{:S(2)}) async-start(bf16[32,4,256]{2,0,1:T(8,128)(2,1)} %bitcast.182), calls=%async_computation | async-start | bytes 131072 | tf_op jit(solution)/shard_map/all_to_all | solution.py:112
  16.2 7.4 %all-to-all-start.2 = ((bf16[32,4,256]{2,0,1:T(8,128)(2,1)}), bf16[32,4,256]{2,0,1:T(8,128)(2,1)S(1)}, u32[]{:S(2)}, u32[]{:S(2)}) async-start(bf16[32,4,256]{2,0,1:T(8,128)(2,1)} %bitcast.181), calls=%async_computation.2 | async-start | bytes 131072 | tf_op jit(solution)/shard_map/all_to_all | solution.py:113
  23.6 24.9 %all-to-all-start.1 = ((bf16[32,4,1536]{2,0,1:T(8,128)(2,1)}), bf16[32,4,1536]{2,0,1:T(8,128)(2,1)S(1)}, u32[]{:S(2)}, u32[]{:S(2)}) async-start(bf16[32,4,1536]{2,0,1:T(8,128)(2,1)} %bitcast.180), calls=%async_computation.1 | async-start | bytes 786432 | tf_op jit(solution)/shard_map/all_to_all | solution.py:111
  40.9 40.3 %collective-permute-start.1 = (s32[1024]{0:T(1024)S(1)}, s32[1024]{0:T(1024)S(1)}, u32[]{:S(2)}, u32[]{:S(2)}) collective-permute-start(s32[1024]{0:T(1024)S(1)} %bitcast.270), channel_id=1, source_target_pairs={{0,1},{1,2},{2,3},{3,4},{4,5},{5,6},{6,7},{7,8},{8,9},{9,10},{10,1... | collective-permute-start | bytes 12296 | tf_op jit(solution)/shard_map/ppermute | solution.py:11
  48.4 58.6 %all-to-all-start.3 = ((bf16[32,4,1536]{2,0,1:T(8,128)(2,1)}), bf16[32,4,1536]{2,0,1:T(8,128)(2,1)S(1)}, u32[]{:S(2)}, u32[]{:S(2)}) async-start(bf16[32,4,1536]{2,0,1:T(8,128)(2,1)} %bitcast.179), calls=%async_computation.3 | async-start | bytes 786432 | tf_op jit(solution)/shard_map/all_to_all | solution.py:114
  56.0 235.8 %reduce-scatter.2.cloned.1.call-start = ((), (), s32[]{:S(2)}) async-start(), calls=%async_computation.8 | async-start | bytes 1179648 | tf_op jit(solution)/shard_map/reduce_scatter | solution.py:141
  75.8 32.6 %collective-permute-start = (bf16[1024,256]{1,0:T(8,128)(2,1)S(1)}, bf16[1024,256]{1,0:T(8,128)(2,1)S(1)}, u32[]{:S(2)}, u32[]{:S(2)}) collective-permute-start(bf16[1024,256]{1,0:T(8,128)(2,1)S(1)} %all_gather.9), channel_id=1, source_target_pairs={{0,1},{1,2},{2,3},{3,4},{4,5},{5,6},{6,7},{7,8},{8,9},{9,10},{10,1... | collective-permute-start | bytes 1572872 | tf_op jit(solution)/shard_map/ppermute | solution.py:11
  103.2 30.4 %collective-permute-start.2 = (bf16[1024,256]{1,0:T(8,128)(2,1)}, bf16[1024,256]{1,0:T(8,128)(2,1)}, u32[]{:S(2)}, u32[]{:S(2)}) collective-permute-start(bf16[1024,256]{1,0:T(8,128)(2,1)} %all_gather.11), channel_id=1, source_target_pairs={{0,1},{1,2},{2,3},{3,4},{4,5},{5,6},{6,7},{7,8},{8,9},{9,10},{10,1... | collective-permute-start | bytes 1572872 | tf_op jit(solution)/shard_map/ppermute | solution.py:11
  107.5 2.4 copy-start.4
  111.5 0.6 copy-start.3
  113.7 1.5 copy-start.9
  115.2 0.6 copy-start.10
  117.4 0.6 copy-start.3
  119.6 1.5 copy-start.9
  121.1 0.6 copy-start.10
  123.3 0.6 copy-start.3
  125.5 1.5 copy-start.9
  127.0 0.6 copy-start.10
  129.2 0.6 copy-start.3
  131.4 1.5 copy-start.9
  132.9 0.6 copy-start.10
  133.5 2.8 copy-start.11
  133.5 2.8 copy-start.7
  136.3 16.6 %copy-start.5 = (bf16[128,2,6,128]{3,2,1,0:T(8,128)(2,1)S(1)}, bf16[128,2,6,128]{3,2,1,0:T(8,128)(2,1)}, u32[]{:S(2)}) copy-start(bf16[128,2,6,128]{3,2,1,0:T(8,128)(2,1)} %copy-done.4) | copy-start | bytes 1179652
  136.3 17.4 %copy-start.2 = (f32[128,2,6,128]{0,3,2,1:T(8,128)S(1)}, f32[128,2,6,128]{0,3,2,1:T(8,128)}, u32[]{:S(2)}) copy-start(f32[128,2,6,128]{0,3,2,1:T(8,128)} %custom-call.3) | copy-start | bytes 2359300
  153.7 4.9 %copy-start.8 = (bf16[128,2,6,128]{3,0,2,1:T(8,128)(2,1)S(1)}, bf16[128,2,6,128]{3,0,2,1:T(8,128)(2,1)}, u32[]{:S(2)}) copy-start(bf16[128,2,6,128]{3,0,2,1:T(8,128)(2,1)} %get-tuple-element.961) | copy-start | bytes 1179652 | tf_op jit(solution)/shard_map/while
  156.9 1.7 copy-start
  162.0 2.0 copy-start.1
  165.4 4.9 %copy-start.8 = (bf16[128,2,6,128]{3,0,2,1:T(8,128)(2,1)S(1)}, bf16[128,2,6,128]{3,0,2,1:T(8,128)(2,1)}, u32[]{:S(2)}) copy-start(bf16[128,2,6,128]{3,0,2,1:T(8,128)(2,1)} %get-tuple-element.961) | copy-start | bytes 1179652 | tf_op jit(solution)/shard_map/while
  168.5 1.7 copy-start
  173.6 2.0 copy-start.1
  177.1 4.9 %copy-start.8 = (bf16[128,2,6,128]{3,0,2,1:T(8,128)(2,1)S(1)}, bf16[128,2,6,128]{3,0,2,1:T(8,128)(2,1)}, u32[]{:S(2)}) copy-start(bf16[128,2,6,128]{3,0,2,1:T(8,128)(2,1)} %get-tuple-element.961) | copy-start | bytes 1179652 | tf_op jit(solution)/shard_map/while
  180.2 1.7 copy-start
  185.3 2.0 copy-start.1
  188.7 4.9 %copy-start.8 = (bf16[128,2,6,128]{3,0,2,1:T(8,128)(2,1)S(1)}, bf16[128,2,6,128]{3,0,2,1:T(8,128)(2,1)}, u32[]{:S(2)}) copy-start(bf16[128,2,6,128]{3,0,2,1:T(8,128)(2,1)} %get-tuple-element.961) | copy-start | bytes 1179652 | tf_op jit(solution)/shard_map/while
  191.9 1.7 copy-start
  197.0 2.0 copy-start.1
  200.4 4.3 %copy-start.6 = (f32[4,512,2,128]{3,1,2,0:T(8,128)S(1)}, f32[4,512,2,128]{3,1,2,0:T(8,128)}, u32[]{:S(2)}) copy-start(f32[4,512,2,128]{3,1,2,0:T(8,128)} %get-tuple-element.389) | copy-start | bytes 6291460
  202.5 38.6 %collective-permute-start.3 = (bf16[1024,256]{1,0:T(8,128)(2,1)S(1)}, bf16[1024,256]{1,0:T(8,128)(2,1)S(1)}, u32[]{:S(2)}, u32[]{:S(2)}) collective-permute-start(bf16[1024,256]{1,0:T(8,128)(2,1)S(1)} %bitcast.250), channel_id=1, source_target_pairs={{1,0},{2,1},{3,2},{4,3},{5,4},{6,5},{7,6},{8,7},{9,8},{10,9},{11,1... | collective-permute-start | bytes 1572872 | tf_op jit(solution)/shard_map/ppermute | solution.py:17
  205.4 46.9 %collective-permute-start.4 = (bf16[1024,256]{1,0:T(8,128)(2,1)S(1)}, bf16[1024,256]{1,0:T(8,128)(2,1)S(1)}, u32[]{:S(2)}, u32[]{:S(2)}) collective-permute-start(bf16[1024,256]{1,0:T(8,128)(2,1)S(1)} %bitcast.251), channel_id=1, source_target_pairs={{1,0},{2,1},{3,2},{4,3},{5,4},{6,5},{7,6},{8,7},{9,8},{10,9},{11,1... | collective-permute-start | bytes 1572872 | tf_op jit(solution)/shard_map/ppermute | solution.py:17
  255.3 38.0 %all-to-all-start.4 = ((bf16[4,32,1536]{2,1,0:T(8,128)(2,1)}), bf16[4,32,1536]{2,1,0:T(8,128)(2,1)S(1)}, u32[]{:S(2)}, u32[]{:S(2)}) async-start(bf16[4,32,1536]{2,1,0:T(8,128)(2,1)} %all_to_all.108), calls=%async_computation.4 | async-start | bytes 786432 | tf_op jit(solution)/shard_map/all_to_all | solution.py:150
  304.9 7.4 %all-to-all-start.6 = ((bf16[4,32,256]{2,1,0:T(8,128)(2,1)}), bf16[4,32,256]{2,1,0:T(8,128)(2,1)S(1)}, u32[]{:S(2)}, u32[]{:S(2)}) async-start(bf16[4,32,256]{2,1,0:T(8,128)(2,1)} %bitcast.12), calls=%async_computation.7 | async-start | bytes 131072 | tf_op jit(solution)/shard_map/all_to_all | solution.py:152
Sparse Core Ops, SparseCore 0:
  253.7 38.0 reduce-scatter.1
where the time goes:
time: 323 us; the launch traced here: 320 us
  waiting for transfers between devices  76.6 us (24%)
  blocking collectives  65.7 us (20%)
  matrix products  47.9 us (15%)
  starting transfers between devices  47.4 us (15%)
  local copies, waits for them, and re-layouts  35.8 us (11%)
  other arithmetic  31.3 us (10%)
  between operations  14.3 us (4%)
    ppermute x2, waiting for transfers between devices, passed_along_2(): lax.ppermute(value, axis, [(source, source + steps) for source in range(i...  41.6 us
    reduce_scatter x1, waiting for transfers between devices, on_device(): lax.psum_scatter(jnp.concatenate([summed_keys, summed_values], axis=1).as...  29.8 us
    all_gather x1, blocking collectives, on_device(): lax.all_gather(value_rows, 'inner', axis=0, tiled=True)  21.3 us
    all_gather x1, blocking collectives, on_device(): lax.all_gather(key_rows, 'inner', axis=0, tiled=True)  19.8 us
    while x52, local copies, waits for them, and re-layouts  13.1 us
    all_gather x1, blocking collectives, on_device(): lax.all_gather(positions, 'inner', axis=0, tiled=True)  13 us
    dot_general x8, matrix products, scored(): jnp.einsum('qhgd,khd->hgqk', query, key_blk, preferred_element_type=jnp.f...  12.2 us
    ppermute x3, starting transfers between devices, passed_along(): lax.ppermute(value, axis, [(i, (i + by) % peers) for i in range(peers)])  12.1 us
  transfers between devices with their start and end apart: 12, of which 6 were waited for; matrix products, arithmetic and copies ran while one was open for 12% of the time, Pallas kernels for 0%

commit v1 on v0

v1 whole, which is shorter than its diff:
```python
import functools

import jax
import jax.numpy as jnp
from jax import lax
from jax.experimental import pallas as pl
from jax.experimental.pallas import tpu as pltpu
from jax.sharding import PartitionSpec as P

D = 128
RUN = 64
NX = 4
KVH = 8
MESH = pl.DeviceIdType.MESH
NEG = -1e30
SCALE = D ** -0.5
EXP_SCALE = SCALE * 1.4426950408889634
F32 = jnp.float32
BF16 = jnp.bfloat16


def dot(a, b):
    return lax.dot_general(a, b, (((1,), (0,)), ((), ())), preferred_element_type=F32)


def sum8(value):
    rows, width = value.shape
    return jnp.sum(value.reshape(rows // 8, 8, width), axis=0)


def kernel(
    ny, nzh, group,
    q_ref, k_ref, v_ref, go_ref, pos_ref,
    gq_ref, gk_ref, gv_ref,
    kv, qbuf, gbuf, poss, qrow, grow, q_t, g_t, pst, dpst, mst, mrun, lrun, drun, dq_t,
    acc, part, rbuf, prior_out, prior_in, kv_out, gq_out,
    fs, fr, ns, nr, ms, mr, ps, pr, hs, hr, rs, rr, bs, br,
):
    half = ny // 2
    width = group * D
    hd, y, o = lax.axis_index("head"), lax.axis_index("inner"), lax.axis_index("outer")
    zl, c = lax.div(hd, 2), lax.rem(hd, 2)
    zh, x = lax.div(o, NX), lax.rem(o, NX)
    xc, s = lax.div(x, 2), lax.rem(x, 2)
    kvh = zl * NX + x
    own = c == xc
    y_right, y_left = lax.rem(y + 1, ny), lax.rem(y + ny - 1, ny)

    forward = []
    for a in range(2):
        for b in range(NX):
            zl2, x2 = lax.rem(zl + a, 2), lax.rem(x + b, NX)
            forward.append(((zl2 * 2 + xc, y, zh * NX + x2), zl2 * NX + x2, own if a + b == 0 else None))
    back = []
    for i in range(4):
        for s2 in range(2):
            hd2 = lax.rem(hd + i, 4)
            me = (2 * c + s2 == x) if i == 0 else None
            back.append(((hd2, y, zh * NX + 2 * c + s2), hd2, s2, me))
    sibling = hd + 1 - 2 * c
    after = (sibling, y, lax.rem(zh + c, nzh) * NX + x)
    before = (sibling, y, lax.rem(zh + nzh - 1 + c, nzh) * NX + x)
    right, left = (hd, y_right, o), (hd, y_left, o)

    def remote(src, dst, send, recv, device):
        return pltpu.make_async_remote_copy(
            src_ref=src, dst_ref=dst, send_sem=send, recv_sem=recv, device_id=device, device_id_type=MESH
        )

    def start(src, dst, send, recv, device, me):
        if me is None:
            remote(src, dst, send, recv, device).start()
        else:
            @pl.when(me)
            def _():
                pltpu.make_async_copy(src, dst, recv).start()

            @pl.when(jnp.logical_not(me))
            def _():
                remote(src, dst, send, recv, device).start()

    def wait_send(src, dst, send, recv, device, me):
        if me is None:
            remote(src, dst, send, recv, device).wait_send()
        else:
            @pl.when(jnp.logical_not(me))
            def _():
                remote(src, dst, send, recv, device).wait_send()

    def wait_recv(dst, recv):
        remote(dst, dst, recv, recv, right).wait_recv()

    barrier = pltpu.get_barrier_semaphore()

    def greet(device):
        pl.semaphore_signal(barrier, inc=1, device_id=device, device_id_type=MESH)

    for device, me in [(f[0], f[2]) for f in forward] + [(b[0], b[3]) for b in back]:
        if me is None:
            greet(device)
        else:
            @pl.when(jnp.logical_not(me))
            def _(device=device):
                greet(device)
    for device in (right, left, after, before):
        greet(device)

    run_id = lax.rem(lax.div(pos_ref[...], RUN), 2 * ny).astype(F32)
    poss[...] = jnp.broadcast_to(run_id, poss.shape).astype(BF16)
    pl.semaphore_wait(barrier, 20 - 2 * own.astype(jnp.int32))

    slot = s * 4 + hd
    token_rows = pl.ds(pl.multiple_of(hd * 32, 32), 32)
    kv_rows = pl.ds(pl.multiple_of(128 + s * 128 + hd * 32, 32), 32)

    def pieces(n, kvh2):
        kv_cols = pl.ds(pl.multiple_of(kvh2 * D, D), D)
        q_cols = pl.ds(pl.multiple_of(kvh2 * width, D), width)
        return (
            (k_ref.at[:, kv_cols], kv.at[y, 0, kv_rows, :], fs.at[0, n], fr.at[0, slot]),
            (v_ref.at[:, kv_cols], kv.at[y, 1, kv_rows, :], fs.at[1, n], fr.at[1, slot]),
            (q_ref.at[:, q_cols], qbuf.at[s, token_rows, :], fs.at[2, n], fr.at[2, slot]),
            (go_ref.at[:, q_cols], gbuf.at[s, token_rows, :], fs.at[3, n], fr.at[3, slot]),
            (poss, kv.at[y, s, pl.ds(384, 16), :], fs.at[4, n], fr.at[4, s]),
        )

    for arrays in ((0, 1), (2, 3)):
        for n, (device, kvh2, me) in enumerate(forward):
            for array in arrays:
                start(*pieces(n, kvh2)[array], device, me)
        if arrays[0] == 0:
            @pl.when(hd == 0)
            def _():
                for n, (device, kvh2, me) in enumerate(forward):
                    start(*pieces(n, kvh2)[4], device, me)

    def wait_kv(s2):
        for hd2 in range(4):
            rows = pl.ds(128 + s2 * 128 + hd2 * 32, 32)
            for which in range(2):
                wait_recv(kv.at[y, which, rows, :], fr.at[which, s2 * 4 + hd2])
        wait_recv(kv.at[y, s2, pl.ds(384, 16), :], fr.at[4, s2])

    wait_kv(1)
    onward = (kv.at[y, :, pl.ds(256, 128), :], kv.at[y, :, pl.ds(0, 128), :], ns.at[0], nr.at[0], after)
    remote(*onward).start()
    wait_kv(0)

    def ring_copy(way, d, part_id):
        origin = lax.rem(y + ny + (1 - d if way == 0 else d - 1), ny)
        device = right if way == 0 else left
        if d == half:
            view = kv.at[origin, way]
            return remote(view, view, hs.at[way], hr.at[way], device)
        view = kv.at[origin, :, pl.ds(128, 272), :] if part_id == 0 else kv.at[origin, :, pl.ds(0, 128), :]
        send, recv = (ms, mr) if part_id == 0 else (ps, pr)
        return remote(view, view, send.at[way, d - 1], recv.at[way, d - 1], device)

    def ring_wait(way, d, part_id):
        origin = lax.rem(y + ny + (-d if way == 0 else d), ny)
        if d == half:
            wait_recv(kv.at[origin, way], hr.at[way])
            return
        view = kv.at[origin, :, pl.ds(128, 272), :] if part_id == 0 else kv.at[origin, :, pl.ds(0, 128), :]
        wait_recv(view, (mr if part_id == 0 else pr).at[way, d - 1])

    def ring_step(d):
        if d == half:
            ring_wait(0, d, 0)
            ring_wait(1, d, 0)
            return
        for part_id in range(2):
            for way in range(2):
                ring_wait(way, d, part_id)
                if d + 1 < half:
                    ring_copy(way, d + 1, part_id).start()
                elif part_id == 1:
                    ring_copy(way, d + 1, 0).start()

    ring_copy(0, 1, 0).start()
    ring_copy(1, 1, 0).start()
    wait_recv(kv.at[y, :, pl.ds(0, 128), :], nr.at[0])
    ring_copy(0, 1, 1).start()
    ring_copy(1, 1, 1).start()
    ring_step(1)

    for s2 in range(2):
        for hd2 in range(4):
            wait_recv(qbuf.at[s2, pl.ds(hd2 * 32, 32), :], fr.at[2, s2 * 4 + hd2])
            wait_recv(gbuf.at[s2, pl.ds(hd2 * 32, 32), :], fr.at[3, s2 * 4 + hd2])
        for g in range(group):
            cols = slice(g * D, (g + 1) * D)
            for src, rows_ref, t_ref in ((qbuf, qrow, q_t), (gbuf, grow, g_t)):
                piece = src[s2, :, cols]
                rows_ref[s2, cols, :] = piece
                t_ref[s2, :, cols] = piece.T

    mrun[...] = jnp.full(mrun.shape, NEG, F32)
    lrun[...] = jnp.zeros(lrun.shape, F32)
    drun[...] = jnp.zeros(drun.shape, F32)
    dq_t[...] = jnp.zeros(dq_t.shape, F32)

    first = jnp.logical_and(c == 0, zh == 0)
    penalties = (jnp.where(first, -NEG, 0.0), None)
    key_off = lax.rem(lax.broadcasted_iota(jnp.int32, (128, 128), 0), RUN).astype(F32)
    row_off = lax.rem(lax.broadcasted_iota(jnp.int32, (8, 128), 1), RUN).astype(F32)

    def forward_chunk(origin):
        for qb in range(2):
            keys = kv[origin, 0, pl.ds(qb * 128, 256), :]
            vals = kv[origin, 1, pl.ds(qb * 128, 256), :]
            scores = dot(keys, q_t[qb])
            dprobs = dot(vals, g_t[qb])
            dpst[origin, qb] = dprobs
            runs = kv[origin, qb, pl.ds(384, 16), :].astype(F32)[:1, :]
            key_pos = jnp.broadcast_to(runs, (128, 128)).T * RUN + key_off
            row_runs = kv[y, qb, pl.ds(384, 16), :].astype(F32)[:1, :]
            allowed = key_pos <= row_runs * RUN + row_off[:1, :]
            prior = scores[:128]
            near = jnp.concatenate(
                [jnp.where(allowed, scores[128:, g * D:(g + 1) * D], NEG) for g in range(group)], axis=1
            )
            prior_top = jnp.max(prior, axis=0, keepdims=True)
            if penalties[qb] is not None:
                prior_top = prior_top - penalties[qb]
            old = mrun[qb]
            top = jnp.maximum(old, jnp.maximum(prior_top, jnp.max(near, axis=0, keepdims=True)))
            mrun[qb] = top
            mst[origin, qb] = top
            shift = top * EXP_SCALE
            prior_shift = shift if penalties[qb] is None else shift + penalties[qb]
            probs = jnp.concatenate(
                [jnp.exp2(prior * EXP_SCALE - prior_shift), jnp.exp2(near * EXP_SCALE - shift)], axis=0
            )
            faded = jnp.exp2((old - top) * EXP_SCALE)
            lrun[qb] = lrun[qb] * faded + sum8(probs)
            drun[qb] = drun[qb] * faded + sum8(probs * dprobs)
            pst[origin, qb] = probs.astype(BF16)

    def chunk_at(d, j):
        return lax.rem(y + ny + (1 - 2 * j) * d, ny)

    def pair(d, work):
        lax.fori_loop(0, 2, lambda j, _: (work(j, chunk_at(d, j)), 0)[1], 0)

    forward_chunk(y)
    pair(1, lambda j, origin: forward_chunk(origin))
    for d in range(2, half):
        ring_step(d)
        pair(d, lambda j, origin: forward_chunk(origin))
    ring_step(half)
    forward_chunk(chunk_at(half, 0))

    for qb in range(2):
        inverse = 1.0 / jnp.sum(lrun[qb], axis=0, keepdims=True)
        delta = jnp.sum(drun[qb], axis=0, keepdims=True) * inverse
        lrun[qb] = jnp.broadcast_to(inverse, lrun.shape[1:])
        drun[qb] = jnp.broadcast_to(delta, drun.shape[1:])

    def backward_chunk(j, origin):
        terms = []
        for qb in range(2):
            weight = jnp.exp2((mst[origin, qb] - mrun[qb]) * EXP_SCALE) * lrun[qb, :1, :]
            probs = pst[origin, qb].astype(F32) * weight
            dscores = (probs * (dpst[origin, qb] - drun[qb, :1, :])).astype(BF16)
            value_term = dot(probs.astype(BF16), grow[qb])
            key_term = dot(dscores, qrow[qb]) * SCALE
            keys = kv[origin, 0, pl.ds(qb * 128, 256), :]
            dq_t[qb] += dot(keys.T, dscores)
            terms.append((key_term, value_term))
        for which in range(2):
            one, two = terms[0][which], terms[1][which]
            acc[j, which, :128, :] = one[:128]
            acc[j, which, 128:256, :] = one[128:] + two[:128]
            acc[j, which, 256:, :] = two[128:]

    backward_chunk(0, chunk_at(half, 0))
    part[0, 0] = acc[0].astype(BF16)
    opposite = [
        remote(part.at[0, 0, way], rbuf.at[way, 0, way], rs.at[way, 0], rr.at[way, 0], right if way == 0 else left)
        for way in range(2)
    ]
    for copy in opposite:
        copy.start()
    steps = []
    for n in range(1, half):
        pair(half - n, backward_chunk)
        for way in range(2):
            if n == 1:
                wait_recv(rbuf.at[way, 0, way], rr.at[way, 0])
                part[way, n, way] = (acc[way, way] + rbuf[way, 0, way].astype(F32)).astype(BF16)
                part[way, n, 1 - way] = acc[way, 1 - way].astype(BF16)
            else:
                wait_recv(rbuf.at[way, n - 1], rr.at[way, n - 1])
                part[way, n] = (acc[way] + rbuf[way, n - 1].astype(F32)).astype(BF16)
            copy = remote(
                part.at[way, n], rbuf.at[way, n], rs.at[way, n], rr.at[way, n], right if way == 0 else left
            )
            copy.start()
            steps.append(copy)
    backward_chunk(0, y)

    for s2 in range(2):
        for g in range(group):
            cols = slice(g * D, (g + 1) * D)
            gq_out[s2, :, cols] = (dq_t[s2, :, cols].T * SCALE).astype(BF16)
    q_cols = pl.ds(pl.multiple_of(kvh * width, D), width)
    kv_cols = pl.ds(pl.multiple_of(kvh * D, D), D)

    def back_pieces(n, hd2, s2):
        rows = pl.ds(pl.multiple_of(hd2 * 32, 32), 32)
        return (
            (kv_out.at[0, s2, rows, :], gk_ref.at[:, kv_cols], bs.at[0, n], br.at[0, kvh]),
            (kv_out.at[1, s2, rows, :], gv_ref.at[:, kv_cols], bs.at[1, n], br.at[1, kvh]),
            (gq_out.at[s2, rows, :], gq_ref.at[:, q_cols], bs.at[2, n], br.at[2, kvh]),
        )

    for n, (device, hd2, s2, me) in enumerate(back):
        start(*back_pieces(n, hd2, s2)[2], device, me)

    for way in range(2):
        wait_recv(rbuf.at[way, half - 1], rr.at[way, half - 1])
    total = acc[0] + rbuf[0, half - 1].astype(F32) + rbuf[1, half - 1].astype(F32)
    prior_out[...] = total[:, :128].astype(BF16)
    prior_copy = remote(prior_out, prior_in, ns.at[1], nr.at[1], before)
    prior_copy.start()
    kv_out[:, 0] = total[:, 128:256].astype(BF16)
    acc[0, :, 256:, :] = total[:, 256:]
    for slot2 in range(2):
        if slot2 == 1:
            prior_copy.wait_recv()
            kv_out[:, 1] = (acc[0, :, 256:, :] + prior_in[...].astype(F32)).astype(BF16)
        for n, (device, hd2, s2, me) in enumerate(back):
            if s2 == slot2:
                for array in range(2):
                    start(*back_pieces(n, hd2, s2)[array], device, me)

    for n, (device, kvh2, me) in enumerate(forward):
        for array in range(4):
            wait_send(*pieces(n, kvh2)[array], device, me)

    @pl.when(hd == 0)
    def _():
        for n, (device, kvh2, me) in enumerate(forward):
            wait_send(*pieces(n, kvh2)[4], device, me)

    for d in range(1, half):
        for way in range(2):
            for part_id in range(2):
                ring_copy(way, d, part_id).wait_send()
    for way in range(2):
        ring_copy(way, half, 0).wait_send()
    for copy in opposite + steps + [remote(*onward), prior_copy]:
        copy.wait_send()
    for n, (device, hd2, s2, me) in enumerate(back):
        for array in range(3):
            wait_send(*back_pieces(n, hd2, s2)[array], device, me)
    for kvh2 in range(KVH):
        wait_recv(gk_ref.at[:, pl.ds(kvh2 * D, D)], br.at[0, kvh2])
        wait_recv(gv_ref.at[:, pl.ds(kvh2 * D, D)], br.at[1, kvh2])
        wait_recv(gq_ref.at[:, pl.ds(kvh2 * width, width)], br.at[2, kvh2])


def on_device(queries, keys, values, grad_out, positions):
    ny, nzh = lax.axis_size("inner"), lax.axis_size("outer") // NX
    rows, width = queries.shape
    group = width // (KVH * D)
    half = ny // 2
    lanes = group * D
    anywhere = pl.BlockSpec(memory_space=pl.ANY)
    vmem = pl.BlockSpec(memory_space=pltpu.VMEM)
    dma = pltpu.SemaphoreType.DMA
    return pl.pallas_call(
        functools.partial(kernel, ny, nzh, group),
        out_shape=tuple(jax.ShapeDtypeStruct(a.shape, BF16) for a in (queries, keys, values)),
        in_specs=[anywhere] * 4 + [vmem],
        out_specs=(anywhere,) * 3,
        scratch_shapes=[
            pltpu.VMEM((ny, 2, 400, D), BF16),
            pltpu.VMEM((2, 128, lanes), BF16),
            pltpu.VMEM((2, 128, lanes), BF16),
            pltpu.VMEM((16, 128), BF16),
            pltpu.VMEM((2, lanes, D), BF16),
            pltpu.VMEM((2, lanes, D), BF16),
            pltpu.VMEM((2, D, lanes), BF16),
            pltpu.VMEM((2, D, lanes), BF16),
            pltpu.VMEM((ny, 2, 256, lanes), BF16),
            pltpu.VMEM((ny, 2, 256, lanes), F32),
            pltpu.VMEM((ny, 2, 1, lanes), F32),
            pltpu.VMEM((2, 1, lanes), F32),
            pltpu.VMEM((2, 8, lanes), F32),
            pltpu.VMEM((2, 8, lanes), F32),
            pltpu.VMEM((2, D, lanes), F32),
            pltpu.VMEM((2, 2, 384, D), F32),
            pltpu.VMEM((2, half, 2, 384, D), BF16),
            pltpu.VMEM((2, half, 2, 384, D), BF16),
            pltpu.VMEM((2, 128, D), BF16),
            pltpu.VMEM((2, 128, D), BF16),
            pltpu.VMEM((2, 2, 128, D), BF16),
            pltpu.VMEM((2, 128, lanes), BF16),
            dma((5, 8)), dma((5, 8)),
            dma((2,)), dma((2,)),
            dma((2, half)), dma((2, half)),
            dma((2, half)), dma((2, half)),
            dma((2,)), dma((2,)),
            dma((2, half)), dma((2, half)),
            dma((3, 8)), dma((3, 8)),
        ],
        compiler_params=pltpu.CompilerParams(
            collective_id=0, has_side_effects=True, vmem_limit_bytes=56 * 1024 * 1024
        ),
        name="banded_backward",
    )(queries, keys, values, grad_out, positions.reshape(1, -1))


def solution(mesh):
    tokens = P(("outer", "inner", "head"), None)
    return jax.shard_map(
        on_device,
        mesh=mesh,
        in_specs=(tokens, tokens, tokens, tokens, P(("outer", "inner"))),
        out_specs=(tokens, tokens, tokens),
        check_vma=False,
    )
```

time: 323 us -> 77.8 us (0.24)
  the two profiles are of different devices: /device:TPU:7 before, /device:TPU:1 now
where the time goes in v1:
time: 77.8 us; the launch traced here: 77.6 us
  Pallas kernels  73.6 us (95%)
  local copies, waits for them, and re-layouts  3.29 us (4%)
    pallas_call x1, Pallas kernels, on_device(): pl.pallas_call(functools.partial(kernel, ny, nzh, group), out_shape=tuple...  73.6 us
    unnamed x7, local copies, waits for them, and re-layouts  3.29 us

profile of v1, /device:TPU:1, one launch (start us, length us, event | category | flops | bytes accessed | tf_op | source)
XLA Modules:
  0.0 77.6 jit_solution(12775701656376581044)
XLA Ops:
  0.6 73.6 %banded_backward.1 = (bf16[32,6144]{1,0:T(8,128)(2,1)}, bf16[32,1024]{1,0:T(8,128)(2,1)}, bf16[32,1024]{1,0:T(8,128)(2,1)}) custom-call(bf16[32,6144]{1,0:T(8,128)(2,1)} %q_ref.1, bf16[32,1024]{1,0:T(8,128)(2,1)} %k_ref.1, bf16[32,1024]{1,0:T(8,128)(2,1)} %v_ref.1, bf16[32,6144]{1,0:T(8,128)(2,1)} %go_ref.1, s32[1,128]{1,0:T(1,128)} %bitcast.1), custom_call_target="tpu_custom_call" | custom-call | tf_op jit(solution)/shard_map/banded_backward/pallas_call | solution.py:373
  74.3 0.0 copy-start.1
  74.3 1.8 %copy.11 = bf16[32,6144]{1,0:T(8,128)(2,1)} copy(bf16[32,6144]{1,0:T(8,128)(2,1)} %get-tuple-element.6) | data formatting | bytes 786432
  76.1 0.0 copy-done.1
  76.1 0.0 copy-start
  76.1 0.6 copy.12
  76.7 0.2 copy-done
  76.9 0.6 copy.13
Async XLA Ops:
  74.3 1.8 %copy-start.1 = (bf16[32,1024]{1,0:T(8,128)(2,1)S(1)}, bf16[32,1024]{1,0:T(8,128)(2,1)}, u32[]{:S(2)}) copy-start(bf16[32,1024]{1,0:T(8,128)(2,1)} %get-tuple-element.7) | copy-start | bytes 196612
  76.1 0.9 %copy-start = (bf16[32,1024]{1,0:T(8,128)(2,1)S(1)}, bf16[32,1024]{1,0:T(8,128)(2,1)}, u32[]{:S(2)}) copy-start(bf16[32,1024]{1,0:T(8,128)(2,1)} %get-tuple-element.8) | copy-start | bytes 196612

commit v2 on v1

v2 whole, which is shorter than its diff:
```python
import functools

import jax
import jax.numpy as jnp
from jax import lax
from jax.experimental import pallas as pl
from jax.experimental.pallas import tpu as pltpu
from jax.sharding import PartitionSpec as P

D = 128
RUN = 64
NX = 4
KVH = 8
MESH = pl.DeviceIdType.MESH
NEG = -1e30
SCALE = D ** -0.5
EXP_SCALE = SCALE * 1.4426950408889634
F32 = jnp.float32
BF16 = jnp.bfloat16


def dot(a, b):
    return lax.dot_general(a, b, (((1,), (0,)), ((), ())), preferred_element_type=F32)


def sum8(value):
    rows, width = value.shape
    return jnp.sum(value.reshape(rows // 8, 8, width), axis=0)


def kernel(
    ny, nzh, group,
    q_ref, k_ref, v_ref, go_ref, pos_ref,
    gq_ref, gk_ref, gv_ref,
    kst, vst, staged, poss, kv, qbuf, gbuf, qrow, grow, q_t, g_t, pst, dpst, mst, mrun, lrun, drun, dq_t,
    acc, part, rbuf, sib_out, sib_in, kv_out, kv_in, prior_in, gq_out,
    ls, fs, fr, os, orr, ks, hs, hr, rs, rr, ss, sr, bs, br, ps, pr,
):
    half = ny // 2
    width = group * D
    hd, y, o = lax.axis_index("head"), lax.axis_index("inner"), lax.axis_index("outer")
    zl, c = lax.div(hd, 2), lax.rem(hd, 2)
    zh, x = lax.div(o, NX), lax.rem(o, NX)
    xc, s = lax.div(x, 2), lax.rem(x, 2)
    kvh = zl * NX + x
    own = c == xc
    core0, core1, last_x = c == 0, c == 1, x == NX - 1

    forward = []
    for a in range(2):
        for b in range(NX):
            zl2, x2 = lax.rem(zl + a, 2), lax.rem(x + b, NX)
            forward.append(((zl2 * 2 + xc, y, zh * NX + x2), zl2 * NX + x2, x2, own if a + b == 0 else None))
    back = []
    for i in range(4):
        for s2 in range(2):
            hd2 = lax.rem(hd + i, 4)
            me = (2 * c + s2 == x) if i == 0 else None
            back.append(((hd2, y, zh * NX + 2 * c + s2), hd2, s2, me))
    zh_after, zh_before = lax.rem(zh + 1, nzh), lax.rem(zh + nzh - 1, nzh)
    heirs = [((2 * zl2, y, zh_after * NX + x2), zl2 * NX + x2) for zl2 in range(2) for x2 in range(NX)]
    donors = [((hd2, y, zh_before * NX + NX - 1), hd2) for hd2 in range(4)]
    sibling = (hd + 1 - 2 * c, y, o)
    ring = ((hd, lax.rem(y + 1, ny), o), (hd, lax.rem(y + ny - 1, ny), o))

    def remote(src, dst, send, recv, device):
        return pltpu.make_async_remote_copy(
            src_ref=src, dst_ref=dst, send_sem=send, recv_sem=recv, device_id=device, device_id_type=MESH
        )

    def wait_recv(dst, recv):
        remote(dst, dst, recv, recv, ring[0]).wait_recv()

    sent = []

    def send(src, dst, send_sem, recv_sem, device, me=None):
        copy = remote(src, dst, send_sem, recv_sem, device)
        if me is None:
            copy.start()
            sent.append((copy, None))
        else:
            @pl.when(me)
            def _():
                pltpu.make_async_copy(src, dst, recv_sem).start()

            away = jnp.logical_not(me)

            @pl.when(away)
            def _():
                copy.start()

            sent.append((copy, away))

    def send_if(condition, *copies):
        copies = [remote(*copy) for copy in copies]

        @pl.when(condition)
        def _():
            for copy in copies:
                copy.start()

        sent.extend((copy, condition) for copy in copies)

    barrier = pltpu.get_barrier_semaphore()

    def greet(device):
        pl.semaphore_signal(barrier, inc=1, device_id=device, device_id_type=MESH)

    @pl.when(last_x)
    def _():
        for device, _ in heirs:
            greet(device)

    @pl.when(core0)
    def _():
        for device, _ in donors:
            greet(device)

    for device, me in [(f[0], f[3]) for f in forward] + [(b[0], b[3]) for b in back]:
        if me is None:
            greet(device)
        else:
            @pl.when(jnp.logical_not(me))
            def _(device=device):
                greet(device)
    for device in ring:
        greet(device)

    loads = [pltpu.make_async_copy(src, dst, ls.at[i]) for i, (src, dst) in enumerate(((k_ref, kst), (v_ref, vst)))]
    for load in loads:
        load.start()
    run_id = lax.rem(lax.div(pos_ref[...], RUN), 2 * ny).astype(F32)
    poss[...] = jnp.broadcast_to(run_id, poss.shape).astype(BF16)
    for load in loads:
        load.wait()
    for h in range(KVH):
        staged[h, :32, :] = kst[:, h * D:(h + 1) * D]
        staged[h, 32:, :] = vst[:, h * D:(h + 1) * D]
    mrun[...] = jnp.full(mrun.shape, NEG, F32)
    lrun[...] = jnp.zeros(lrun.shape, F32)
    drun[...] = jnp.zeros(drun.shape, F32)
    dq_t[...] = jnp.zeros(dq_t.shape, F32)
    pl.semaphore_wait(
        barrier,
        18 - 2 * own.astype(jnp.int32) + 8 * last_x.astype(jnp.int32) + 4 * core0.astype(jnp.int32),
    )

    kv_rows = pl.ds(pl.multiple_of(hd * 64, 64), 64)
    for n, (device, kvh2, x2, me) in enumerate(forward):
        send(staged.at[kvh2], kv.at[y, 1 + s, kv_rows, :], fs.at[0, n], fr.at[0, s * 4 + hd], device, me)
    send_if(last_x, *(
        (staged.at[kvh2], kv.at[y, 0, kv_rows, :], os.at[n], orr.at[hd], device)
        for n, (device, kvh2) in enumerate(heirs)
    ))
    for n, (device, kvh2, x2, me) in enumerate(forward):
        runs = (poss, kv.at[y, 1 + s, pl.ds(256, 16), :], fs.at[3, n], fr.at[3, s], device)
        mine = x2 == hd
        if me is None:
            send_if(mine, runs)
        else:
            @pl.when(jnp.logical_and(mine, me))
            def _(runs=runs):
                pltpu.make_async_copy(runs[0], runs[1], runs[3]).start()

            send_if(jnp.logical_and(mine, jnp.logical_not(me)), runs)

    def view(origin, p, d, way):
        rows = pl.ds(0, 272 if p else 256)
        if d == half:
            rows = pl.ds(0, 128) if way == 0 else pl.ds(128, 144 if p else 128)
        return kv.at[origin, p, rows, :]

    def origin_at(way, d):
        return lax.rem(y + ny + (-d if way == 0 else d), ny)

    def gather_send(way, d, p):
        piece = view(origin_at(way, d - 1), p, d, way)
        copy = (piece, piece, hs.at[way, d - 1, p], hr.at[way, d - 1, p], ring[way])
        if p == 0:
            send_if(core0, copy)
        else:
            send(*copy)

    def hand_over(way, d):
        origin = origin_at(way, d)
        rows = pl.ds(0, 256) if d < half else pl.ds(128 * way, 128)
        send_if(core0, (
            kv.at[origin, 2, rows, :], kv.at[origin, 0, rows, :], ks.at[way, d], hr.at[way, d - 1, 0] if d else orr.at[0],
            sibling,
        ))

    def gather_events(d):
        def event(way, p):
            wait_recv(view(origin_at(way, d), p, d, way), hr.at[way, d - 1, p])
            if d < half:
                gather_send(way, d + 1, p)
            if p == 2:
                hand_over(way, d)

        return [functools.partial(event, way, p) for p in (2, 1, 0) for way in range(2)]

    for p in (2, 1):
        for hd2 in range(4):
            wait_recv(kv.at[y, p, pl.ds(hd2 * 64, 64), :], fr.at[0, (p - 1) * 4 + hd2])
        wait_recv(kv.at[y, p, pl.ds(256, 16), :], fr.at[3, p - 1])
        for way in range(2):
            gather_send(way, 1, p)
        if p == 2:
            hand_over(0, 0)

    @pl.when(core0)
    def _():
        for hd2 in range(4):
            wait_recv(kv.at[y, 0, pl.ds(hd2 * 64, 64), :], orr.at[hd2])

    for way in range(2):
        gather_send(way, 1, 0)

    token_rows = pl.ds(pl.multiple_of(hd * 32, 32), 32)
    for n, (device, kvh2, x2, me) in enumerate(forward):
        q_cols = pl.ds(pl.multiple_of(kvh2 * width, D), width)
        send(q_ref.at[:, q_cols], qbuf.at[s, token_rows, :], fs.at[1, n], fr.at[1, s * 4 + hd], device, me)
        send(go_ref.at[:, q_cols], gbuf.at[s, token_rows, :], fs.at[2, n], fr.at[2, s * 4 + hd], device, me)

    for d in range(1, half - 1):
        for event in gather_events(d):
            event()

    @pl.when(core1)
    def _():
        wait_recv(kv.at[y, 0, pl.ds(0, 256), :], orr.at[0])

    for s2 in range(2):
        for hd2 in range(4):
            wait_recv(qbuf.at[s2, pl.ds(hd2 * 32, 32), :], fr.at[1, s2 * 4 + hd2])
            wait_recv(gbuf.at[s2, pl.ds(hd2 * 32, 32), :], fr.at[2, s2 * 4 + hd2])
        for g in range(group):
            cols = slice(g * D, (g + 1) * D)
            for src, rows_ref, t_ref in ((qbuf, qrow, q_t), (gbuf, grow, g_t)):
                piece = src[s2, :, cols]
                rows_ref[s2, cols, :] = piece
                t_ref[s2, :, cols] = piece.T

    first = jnp.logical_and(core0, zh == 0)
    key_off = lax.rem(lax.broadcasted_iota(jnp.int32, (128, 128), 0), RUN).astype(F32)
    row_off = lax.rem(lax.broadcasted_iota(jnp.int32, (8, 128), 1), RUN).astype(F32)

    def rows_of(origin, qb, which):
        at = [pl.ds(hd2 * 64 + which * 32, 32) for hd2 in range(4)]
        return jnp.concatenate([kv[origin, qb + p, rows, :] for p in range(2) for rows in at], axis=0)

    def forward_chunk(origin):
        def block(qb, _):
            scores = dot(rows_of(origin, qb, 0), q_t[qb])
            dprobs = dot(rows_of(origin, qb, 1), g_t[qb])
            dpst[origin, qb] = dprobs
            runs = kv[origin, qb + 1, pl.ds(256, 16), :].astype(F32)[:1, :]
            key_pos = jnp.broadcast_to(runs, (128, 128)).T * RUN + key_off
            row_runs = kv[y, qb + 1, pl.ds(256, 16), :].astype(F32)[:1, :]
            allowed = key_pos <= row_runs * RUN + row_off[:1, :]
            penalty = jnp.where(jnp.logical_and(first, qb == 0), -NEG, 0.0)
            prior = scores[:128]
            near = jnp.concatenate(
                [jnp.where(allowed, scores[128:, g * D:(g + 1) * D], NEG) for g in range(group)], axis=1
            )
            prior_top = jnp.max(prior, axis=0, keepdims=True) - penalty
            old = mrun[qb]
            top = jnp.maximum(old, jnp.maximum(prior_top, jnp.max(near, axis=0, keepdims=True)))
            mrun[qb] = top
            mst[origin, qb] = top
            shift = top * EXP_SCALE
            probs = jnp.concatenate(
                [jnp.exp2(prior * EXP_SCALE - (shift + penalty)), jnp.exp2(near * EXP_SCALE - shift)], axis=0
            )
            faded = jnp.exp2((old - top) * EXP_SCALE)
            lrun[qb] = lrun[qb] * faded + sum8(probs)
            drun[qb] = drun[qb] * faded + sum8(probs * dprobs)
            pst[origin, qb] = probs.astype(BF16)
            return 0

        lax.fori_loop(0, 2, block, 0)

    def chunk_at(d, j):
        return lax.rem(y + ny + (1 - 2 * j) * d, ny)

    chunks = [(0, 0)] + [(d, j) for d in range(1, half - 1) for j in range(2)]
    events = gather_events(half - 1)
    for i, event in enumerate(events):
        event()
        for d, j in chunks[i * len(chunks) // len(events):(i + 1) * len(chunks) // len(events)]:
            forward_chunk(chunk_at(d, j))
    for j in range(2):
        forward_chunk(chunk_at(half - 1, j))
    for event in gather_events(half):
        event()
    forward_chunk(chunk_at(half, 0))

    for qb in range(2):
        inverse = 1.0 / jnp.sum(lrun[qb], axis=0, keepdims=True)
        delta = jnp.sum(drun[qb], axis=0, keepdims=True) * inverse
        lrun[qb] = jnp.broadcast_to(inverse, lrun.shape[1:])
        drun[qb] = jnp.broadcast_to(delta, drun.shape[1:])

    def backward_chunk(d, j):
        origin = chunk_at(d, j)

        def block(qb, _):
            weight = jnp.exp2((mst[origin, qb] - mrun[qb]) * EXP_SCALE) * lrun[qb, :1, :]
            probs = pst[origin, qb].astype(F32) * weight
            dscores = (probs * (dpst[origin, qb] - drun[qb, :1, :])).astype(BF16)
            acc[origin, qb, 0] = dot(dscores, qrow[qb]) * SCALE
            acc[origin, qb, 1] = dot(probs.astype(BF16), grow[qb])
            dq_t[qb] += dot(rows_of(origin, qb, 0).T, dscores)
            return 0

        lax.fori_loop(0, 2, block, 0)

        @pl.when(core1)
        def _():
            sib_out[origin] = acc[origin, 0, :, :128, :].astype(BF16)

        send_if(core1, (sib_out.at[origin], sib_in.at[origin], ss.at[d, j], sr.at[d, j], sibling))

    def term(d, j, p, which):
        origin = chunk_at(d, j)
        if p == 0:
            return acc[origin, 0, which, :128, :]
        if p == 1:
            return acc[origin, 0, which, 128:, :] + acc[origin, 1, which, :128, :]
        mine = acc[origin, 1, which, 128:, :]
        return mine + jnp.where(core0, sib_in[origin, which].astype(F32), 0.0)

    def from_sibling(d, j):
        @pl.when(core0)
        def _():
            wait_recv(sib_in.at[chunk_at(d, j)], sr.at[d, j])

    def scatter(n, way, p):
        d = half - n
        if n == 1:
            wait_recv(rbuf.at[way, 0, p, way], rr.at[way, 0, p])
        elif n > 1:
            wait_recv(rbuf.at[way, n - 1, p], rr.at[way, n - 1, p])
        for which in range(2):
            if n == 0 and which != way:
                continue
            total = term(d, way if n else 0, p, which)
            if n > 1 or n == 1 and which == way:
                total = total + rbuf[way, n - 1, p, which].astype(F32)
            part[way, n, p, which] = total.astype(BF16)

    def scatter_events(n):
        def event(way, p):
            if p == 2 and (n or not way):
                from_sibling(half - n, way)
            at = (way, n, p) if n else (way, n, p, way)
            copy = (part.at[at], rbuf.at[at], rs.at[way, n, p], rr.at[way, n, p], ring[way])
            if p == 0:
                @pl.when(core0)
                def _():
                    scatter(n, way, p)

                send_if(core0, copy)
            else:
                scatter(n, way, p)
                send(*copy)

        return [functools.partial(event, way, p) for p in range(3) for way in range(2)]

    backward_chunk(half, 0)
    for event in scatter_events(0):
        event()
    for n in range(1, half):
        for d in (half - 1, half - 2) if n == 1 else (half - n - 1,):
            for j in range(2 if d else 1):
                backward_chunk(d, j)
        if n == half - 1:
            for s2 in range(2):
                for g in range(group):
                    cols = slice(g * D, (g + 1) * D)
                    gq_out[s2, :, cols] = (dq_t[s2, :, cols].T * SCALE).astype(BF16)
            q_cols = pl.ds(pl.multiple_of(kvh * width, D), width)
            for m, (device, hd2, s2, me) in enumerate(back):
                rows = pl.ds(pl.multiple_of(hd2 * 32, 32), 32)
                send(gq_out.at[s2, rows, :], gq_ref.at[:, q_cols], bs.at[1, m], br.at[1, kvh], device, me)
        for event in scatter_events(n):
            event()

    def finish(p):
        for way in range(2):
            wait_recv(rbuf.at[way, half - 1, p], rr.at[way, half - 1, p])
        for which in range(2):
            total = term(0, 0, p, which)
            total = total + rbuf[0, half - 1, p, which].astype(F32) + rbuf[1, half - 1, p, which].astype(F32)
            for hd2 in range(4):
                kv_out[p, hd2, pl.ds(which * 32, 32), :] = total[hd2 * 32:(hd2 + 1) * 32].astype(BF16)

    @pl.when(core0)
    def _():
        finish(0)

    send_if(core0, *(
        (kv_out.at[0, hd2], prior_in.at[kvh], ps.at[hd2], pr.at[kvh], device) for device, hd2 in donors
    ))
    for p in (1, 2):
        if p == 2:
            from_sibling(0, 0)
        finish(p)
        for m, (device, hd2, s2, me) in enumerate(back):
            if s2 == p - 1:
                send(kv_out.at[p, hd2], kv_in.at[kvh], bs.at[0, m], br.at[0, kvh], device, me)

    def results(with_prior):
        for h in range(KVH):
            both = kv_in[h]
            if with_prior:
                both = (both.astype(F32) + prior_in[h].astype(F32)).astype(BF16)
            cols = slice(h * D, (h + 1) * D)
            gk_ref[:, cols] = both[:32]
            gv_ref[:, cols] = both[32:]

    for h in range(KVH):
        wait_recv(gq_ref.at[:, pl.ds(h * width, width)], br.at[1, h])
        wait_recv(kv_in.at[h], br.at[0, h])

    @pl.when(last_x)
    def _():
        for h in range(KVH):
            wait_recv(prior_in.at[h], pr.at[h])
        results(True)

    @pl.when(jnp.logical_not(last_x))
    def _():
        results(False)

    for copy, condition in sent:
        if condition is None:
            copy.wait_send()
        else:
            @pl.when(condition)
            def _(copy=copy):
                copy.wait_send()


def on_device(queries, keys, values, grad_out, positions):
    ny, nzh = lax.axis_size("inner"), lax.axis_size("outer") // NX
    rows, width = queries.shape
    group = width // (KVH * D)
    half = ny // 2
    lanes = group * D
    anywhere = pl.BlockSpec(memory_space=pl.ANY)
    vmem = pl.BlockSpec(memory_space=pltpu.VMEM)
    dma = pltpu.SemaphoreType.DMA
    return pl.pallas_call(
        functools.partial(kernel, ny, nzh, group),
        out_shape=tuple(jax.ShapeDtypeStruct(a.shape, BF16) for a in (queries, keys, values)),
        in_specs=[anywhere] * 4 + [vmem],
        out_specs=(anywhere, vmem, vmem),
        scratch_shapes=[
            pltpu.VMEM((32, KVH * D), BF16),
            pltpu.VMEM((32, KVH * D), BF16),
            pltpu.VMEM((KVH, 64, D), BF16),
            pltpu.VMEM((16, 128), BF16),
            pltpu.VMEM((ny, 3, 272, D), BF16),
            pltpu.VMEM((2, 128, lanes), BF16),
            pltpu.VMEM((2, 128, lanes), BF16),
            pltpu.VMEM((2, lanes, D), BF16),
            pltpu.VMEM((2, lanes, D), BF16),
            pltpu.VMEM((2, D, lanes), BF16),
            pltpu.VMEM((2, D, lanes), BF16),
            pltpu.VMEM((ny, 2, 256, lanes), BF16),
            pltpu.VMEM((ny, 2, 256, lanes), F32),
            pltpu.VMEM((ny, 2, 1, lanes), F32),
            pltpu.VMEM((2, 1, lanes), F32),
            pltpu.VMEM((2, 8, lanes), F32),
            pltpu.VMEM((2, 8, lanes), F32),
            pltpu.VMEM((2, D, lanes), F32),
            pltpu.VMEM((ny, 2, 2, 256, D), F32),
            pltpu.VMEM((2, half, 3, 2, 128, D), BF16),
            pltpu.VMEM((2, half, 3, 2, 128, D), BF16),
            pltpu.VMEM((ny, 2, 128, D), BF16),
            pltpu.VMEM((ny, 2, 128, D), BF16),
            pltpu.VMEM((3, 4, 64, D), BF16),
            pltpu.VMEM((KVH, 64, D), BF16),
            pltpu.VMEM((KVH, 64, D), BF16),
            pltpu.VMEM((2, 128, lanes), BF16),
            dma((2,)),
            dma((4, 8)), dma((4, 8)),
            dma((8,)), dma((4,)),
            dma((2, half + 1)),
            dma((2, half, 3)), dma((2, half, 3)),
            dma((2, half, 3)), dma((2, half, 3)),
            dma((half + 1, 2)), dma((half + 1, 2)),
            dma((2, 8)), dma((2, 8)),
            dma((4,)), dma((8,)),
        ],
        compiler_params=pltpu.CompilerParams(
            collective_id=0, has_side_effects=True, vmem_limit_bytes=56 * 1024 * 1024
        ),
        name="banded_backward",
    )(queries, keys, values, grad_out, positions.reshape(1, -1))


def solution(mesh):
    tokens = P(("outer", "inner", "head"), None)
    return jax.shard_map(
        on_device,
        mesh=mesh,
        in_specs=(tokens, tokens, tokens, tokens, P(("outer", "inner"))),
        out_specs=(tokens, tokens, tokens),
        check_vma=False,
    )
```

time: 77.8 us -> 74.1 us (0.952)
  Pallas kernels: 73.6 us -> 69.9 us
    pallas_call x1, Pallas kernels: 73.6 us -> 69.9 us  [on_device(): pl.pallas_call(functools.partial(kernel, ny, nzh, group), out_shape=tuple...]
where the time goes in v2:
time: 74.1 us; the launch traced here: 73.9 us
  Pallas kernels  69.9 us (94%)
  local copies, waits for them, and re-layouts  3.29 us (4%)
    pallas_call x1, Pallas kernels, on_device(): pl.pallas_call(functools.partial(kernel, ny, nzh, group), out_shape=tuple...  69.9 us
    unnamed x7, local copies, waits for them, and re-layouts  3.29 us

profile of v2, /device:TPU:1, one launch (start us, length us, event | category | flops | bytes accessed | tf_op | source)
XLA Modules:
  0.0 73.9 jit_solution(3838240635537394849)
XLA Ops:
  0.6 69.9 %banded_backward.1 = (bf16[32,6144]{1,0:T(8,128)(2,1)}, bf16[32,1024]{1,0:T(8,128)(2,1)}, bf16[32,1024]{1,0:T(8,128)(2,1)}) custom-call(bf16[32,6144]{1,0:T(8,128)(2,1)} %q_ref.1, bf16[32,1024]{1,0:T(8,128)(2,1)} %k_ref.1, bf16[32,1024]{1,0:T(8,128)(2,1)} %v_ref.1, bf16[32,6144]{1,0:T(8,128)(2,1)} %go_ref.1, s32[1,128]{1,0:T(1,128)} %bitcast.1), custom_call_target="tpu_custom_call" | custom-call | tf_op jit(solution)/shard_map/banded_backward/pallas_call | solution.py:454
  70.6 0.0 copy-start.1
  70.6 1.8 %copy.11 = bf16[32,6144]{1,0:T(8,128)(2,1)} copy(bf16[32,6144]{1,0:T(8,128)(2,1)} %get-tuple-element.6) | data formatting | bytes 786432
  72.4 0.0 copy-done.1
  72.4 0.0 copy-start
  72.4 0.6 copy.12
  73.0 0.2 copy-done
  73.2 0.6 copy.13
Async XLA Ops:
  70.6 1.8 %copy-start.1 = (bf16[32,1024]{1,0:T(8,128)(2,1)S(1)}, bf16[32,1024]{1,0:T(8,128)(2,1)}, u32[]{:S(2)}) copy-start(bf16[32,1024]{1,0:T(8,128)(2,1)} %get-tuple-element.7) | copy-start | bytes 196612
  72.4 0.9 %copy-start = (bf16[32,1024]{1,0:T(8,128)(2,1)S(1)}, bf16[32,1024]{1,0:T(8,128)(2,1)}, u32[]{:S(2)}) copy-start(bf16[32,1024]{1,0:T(8,128)(2,1)} %get-tuple-element.8) | copy-start | bytes 196612

commit v3 on v2

--- a/solution.py
+++ b/solution.py
@@ -34,7 +34,7 @@
     gq_ref, gk_ref, gv_ref,
     kst, vst, staged, poss, kv, qbuf, gbuf, qrow, grow, q_t, g_t, pst, dpst, mst, mrun, lrun, drun, dq_t,
     acc, part, rbuf, sib_out, sib_in, kv_out, kv_in, prior_in, gq_out,
-    ls, fs, fr, os, orr, ks, hs, hr, rs, rr, ss, sr, bs, br, ps, pr,
+    ls, fs, fr, os, orr, ks, hs, hr, rs, rr, ss, sr, bs, br, ps, pr, ready,
 ):
     half = ny // 2
     width = group * D
@@ -44,7 +44,11 @@
     xc, s = lax.div(x, 2), lax.rem(x, 2)
     kvh = zl * NX + x
     own = c == xc
-    core0, core1, last_x = c == 0, c == 1, x == NX - 1
+    core0, core1 = c == 0, c == 1
+    first = jnp.logical_and(core0, zh == 0)
+    has_prior = jnp.logical_and(core0, zh > 0)
+    gives_prior = jnp.logical_and(core1, zh < nzh - 1)
+    owns_prior = jnp.logical_and(x == NX - 1, zh < nzh - 1)
 
     forward = []
     for a in range(2):
@@ -57,11 +61,12 @@
             hd2 = lax.rem(hd + i, 4)
             me = (2 * c + s2 == x) if i == 0 else None
             back.append(((hd2, y, zh * NX + 2 * c + s2), hd2, s2, me))
-    zh_after, zh_before = lax.rem(zh + 1, nzh), lax.rem(zh + nzh - 1, nzh)
-    heirs = [((2 * zl2, y, zh_after * NX + x2), zl2 * NX + x2) for zl2 in range(2) for x2 in range(NX)]
-    donors = [((hd2, y, zh_before * NX + NX - 1), hd2) for hd2 in range(4)]
+    zh_after, zh_before = jnp.minimum(zh + 1, nzh - 1), jnp.maximum(zh - 1, 0)
     sibling = (hd + 1 - 2 * c, y, o)
+    heir, donor = (sibling[0], y, zh_after * NX + x), (sibling[0], y, zh_before * NX + x)
+    owners = [((hd2, y, zh_before * NX + NX - 1), hd2) for hd2 in range(4)]
     ring = ((hd, lax.rem(y + 1, ny), o), (hd, lax.rem(y + ny - 1, ny), o))
+    ring2 = ((hd, lax.rem(y + 2, ny), o), (hd, lax.rem(y + ny - 2, ny), o))
 
     def remote(src, dst, send, recv, device):
         return pltpu.make_async_remote_copy(
@@ -106,25 +111,30 @@
     def greet(device):
         pl.semaphore_signal(barrier, inc=1, device_id=device, device_id_type=MESH)
 
-    @pl.when(last_x)
-    def _():
-        for device, _ in heirs:
-            greet(device)
-
-    @pl.when(core0)
-    def _():
-        for device, _ in donors:
-            greet(device)
-
-    for device, me in [(f[0], f[3]) for f in forward] + [(b[0], b[3]) for b in back]:
+    @pl.when(has_prior)
+    def _():
+        greet(donor)
+
+    for device, _, _, me in back:
         if me is None:
             greet(device)
         else:
             @pl.when(jnp.logical_not(me))
             def _(device=device):
                 greet(device)
-    for device in ring:
+    for device in ring + ring2:
         greet(device)
+
+    @pl.when(jnp.logical_not(own))
+    def _():
+        greet(sibling)
+
+    @pl.when(owns_prior)
+    def _():
+        for zl2 in range(2):
+            for x2 in range(NX):
+                greet((2 * zl2, y, zh_after * NX + x2))
+
 
     loads = [pltpu.make_async_copy(src, dst, ls.at[i]) for i, (src, dst) in enumerate(((k_ref, kst), (v_ref, vst)))]
     for load in loads:
@@ -136,22 +146,23 @@
     for h in range(KVH):
         staged[h, :32, :] = kst[:, h * D:(h + 1) * D]
         staged[h, 32:, :] = vst[:, h * D:(h + 1) * D]
+    @pl.when(first)
+    def _():
+        for origin in range(ny):
+            kv[origin, 0] = jnp.zeros(kv.shape[2:], BF16)
+
     mrun[...] = jnp.full(mrun.shape, NEG, F32)
     lrun[...] = jnp.zeros(lrun.shape, F32)
     drun[...] = jnp.zeros(drun.shape, F32)
     dq_t[...] = jnp.zeros(dq_t.shape, F32)
     pl.semaphore_wait(
         barrier,
-        18 - 2 * own.astype(jnp.int32) + 8 * last_x.astype(jnp.int32) + 4 * core0.astype(jnp.int32),
+        12 + gives_prior.astype(jnp.int32) + 4 * has_prior.astype(jnp.int32),
     )
 
     kv_rows = pl.ds(pl.multiple_of(hd * 64, 64), 64)
     for n, (device, kvh2, x2, me) in enumerate(forward):
         send(staged.at[kvh2], kv.at[y, 1 + s, kv_rows, :], fs.at[0, n], fr.at[0, s * 4 + hd], device, me)
-    send_if(last_x, *(
-        (staged.at[kvh2], kv.at[y, 0, kv_rows, :], os.at[n], orr.at[hd], device)
-        for n, (device, kvh2) in enumerate(heirs)
-    ))
     for n, (device, kvh2, x2, me) in enumerate(forward):
         runs = (poss, kv.at[y, 1 + s, pl.ds(256, 16), :], fs.at[3, n], fr.at[3, s], device)
         mine = x2 == hd
@@ -173,11 +184,11 @@
     def origin_at(way, d):
         return lax.rem(y + ny + (-d if way == 0 else d), ny)
 
-    def gather_send(way, d, p):
-        piece = view(origin_at(way, d - 1), p, d, way)
-        copy = (piece, piece, hs.at[way, d - 1, p], hr.at[way, d - 1, p], ring[way])
+    def gather_send(way, d, p, far=1):
+        piece = view(origin_at(way, d - far), p, d, way)
+        copy = (piece, piece, hs.at[way, d - 1, p], hr.at[way, d - 1, p], (ring, ring2)[far - 1][way])
         if p == 0:
-            send_if(core0, copy)
+            send_if(has_prior, copy)
         else:
             send(*copy)
 
@@ -185,15 +196,25 @@
         origin = origin_at(way, d)
         rows = pl.ds(0, 256) if d < half else pl.ds(128 * way, 128)
         send_if(core0, (
-            kv.at[origin, 2, rows, :], kv.at[origin, 0, rows, :], ks.at[way, d], hr.at[way, d - 1, 0] if d else orr.at[0],
+            kv.at[origin, 2, rows, :], kv.at[origin, 0, rows, :], ks.at[way, d - 1], hr.at[way, d - 1, 0],
             sibling,
         ))
 
     def gather_events(d):
         def event(way, p):
-            wait_recv(view(origin_at(way, d), p, d, way), hr.at[way, d - 1, p])
-            if d < half:
+            piece = view(origin_at(way, d), p, d, way)
+            if p == 0:
+                @pl.when(jnp.logical_not(first))
+                def _():
+                    wait_recv(piece, hr.at[way, d - 1, p])
+            else:
+                wait_recv(piece, hr.at[way, d - 1, p])
+            if p and d < half:
                 gather_send(way, d + 1, p)
+            if p == 0 and d % 2 == 0:
+                for far in (1, 2):
+                    if d + far <= half:
+                        gather_send(way, d + far, 0, far)
             if p == 2:
                 hand_over(way, d)
 
@@ -206,29 +227,34 @@
         for way in range(2):
             gather_send(way, 1, p)
         if p == 2:
-            hand_over(0, 0)
-
-    @pl.when(core0)
-    def _():
-        for hd2 in range(4):
-            wait_recv(kv.at[y, 0, pl.ds(hd2 * 64, 64), :], orr.at[hd2])
-
-    for way in range(2):
-        gather_send(way, 1, 0)
-
+            block, prior = (kv.at[y, i, pl.ds(0, 256), :] for i in (2, 0))
+            send_if(gives_prior, (block, prior, os, orr, heir))
+            send_if(core0, (block, prior, os, orr, sibling))
     token_rows = pl.ds(pl.multiple_of(hd * 32, 32), 32)
     for n, (device, kvh2, x2, me) in enumerate(forward):
         q_cols = pl.ds(pl.multiple_of(kvh2 * width, D), width)
         send(q_ref.at[:, q_cols], qbuf.at[s, token_rows, :], fs.at[1, n], fr.at[1, s * 4 + hd], device, me)
         send(go_ref.at[:, q_cols], gbuf.at[s, token_rows, :], fs.at[2, n], fr.at[2, s * 4 + hd], device, me)
 
+
+    for device, kvh2, x2, me in forward:
+        if me is None:
+            pl.semaphore_signal(ready, inc=1, device_id=device, device_id_type=MESH)
+        else:
+            @pl.when(jnp.logical_not(me))
+            def _(device=device):
+                pl.semaphore_signal(ready, inc=1, device_id=device, device_id_type=MESH)
+
+    @pl.when(jnp.logical_not(first))
+    def _():
+        wait_recv(kv.at[y, 0, pl.ds(0, 256), :], orr)
+
+    for far in (1, 2):
+        for way in range(2):
+            gather_send(way, far, 0, far)
     for d in range(1, half - 1):
         for event in gather_events(d):
             event()
-
-    @pl.when(core1)
-    def _():
-        wait_recv(kv.at[y, 0, pl.ds(0, 256), :], orr.at[0])
 
     for s2 in range(2):
         for hd2 in range(4):
@@ -241,7 +267,6 @@
                 rows_ref[s2, cols, :] = piece
                 t_ref[s2, :, cols] = piece.T
 
-    first = jnp.logical_and(core0, zh == 0)
     key_off = lax.rem(lax.broadcasted_iota(jnp.int32, (128, 128), 0), RUN).astype(F32)
     row_off = lax.rem(lax.broadcasted_iota(jnp.int32, (8, 128), 1), RUN).astype(F32)
 
@@ -356,11 +381,11 @@
             at = (way, n, p) if n else (way, n, p, way)
             copy = (part.at[at], rbuf.at[at], rs.at[way, n, p], rr.at[way, n, p], ring[way])
             if p == 0:
-                @pl.when(core0)
+                @pl.when(has_prior)
                 def _():
                     scatter(n, way, p)
 
-                send_if(core0, copy)
+                send_if(has_prior, copy)
             else:
                 scatter(n, way, p)
                 send(*copy)
@@ -379,6 +404,7 @@
                 for g in range(group):
                     cols = slice(g * D, (g + 1) * D)
                     gq_out[s2, :, cols] = (dq_t[s2, :, cols].T * SCALE).astype(BF16)
+            pl.semaphore_wait(ready, 8 - own.astype(jnp.int32))
             q_cols = pl.ds(pl.multiple_of(kvh * width, D), width)
             for m, (device, hd2, s2, me) in enumerate(back):
                 rows = pl.ds(pl.multiple_of(hd2 * 32, 32), 32)
@@ -395,12 +421,12 @@
             for hd2 in range(4):
                 kv_out[p, hd2, pl.ds(which * 32, 32), :] = total[hd2 * 32:(hd2 + 1) * 32].astype(BF16)
 
-    @pl.when(core0)
+    @pl.when(has_prior)
     def _():
         finish(0)
 
-    send_if(core0, *(
-        (kv_out.at[0, hd2], prior_in.at[kvh], ps.at[hd2], pr.at[kvh], device) for device, hd2 in donors
+    send_if(has_prior, *(
+        (kv_out.at[0, hd2], prior_in.at[kvh], ps.at[hd2], pr.at[kvh], device) for device, hd2 in owners
     ))
     for p in (1, 2):
         if p == 2:
@@ -423,13 +449,13 @@
         wait_recv(gq_ref.at[:, pl.ds(h * width, width)], br.at[1, h])
         wait_recv(kv_in.at[h], br.at[0, h])
 
-    @pl.when(last_x)
+    @pl.when(owns_prior)
     def _():
         for h in range(KVH):
             wait_recv(prior_in.at[h], pr.at[h])
         results(True)
 
-    @pl.when(jnp.logical_not(last_x))
+    @pl.when(jnp.logical_not(owns_prior))
     def _():
         results(False)
 
@@ -486,13 +512,14 @@
             pltpu.VMEM((2, 128, lanes), BF16),
             dma((2,)),
             dma((4, 8)), dma((4, 8)),
-            dma((8,)), dma((4,)),
-            dma((2, half + 1)),
+            dma, dma,
+            dma((2, half)),
             dma((2, half, 3)), dma((2, half, 3)),
             dma((2, half, 3)), dma((2, half, 3)),
             dma((half + 1, 2)), dma((half + 1, 2)),
             dma((2, 8)), dma((2, 8)),
             dma((4,)), dma((8,)),
+            pltpu.SemaphoreType.REGULAR,
         ],
         compiler_params=pltpu.CompilerParams(
             collective_id=0, has_side_effects=True, vmem_limit_bytes=56 * 1024 * 1024

time: 74.1 us -> 67.6 us (0.912)
  the two profiles are of different devices: /device:TPU:1 before, /device:TPU:7 now
where the time goes in v3:
time: 67.6 us; the launch traced here: 67 us
  Pallas kernels  63.1 us (93%)
  local copies, waits for them, and re-layouts  3.29 us (5%)
    pallas_call x1, Pallas kernels, on_device(): pl.pallas_call(functools.partial(kernel, ny, nzh, group), out_shape=tuple...  63.1 us
    unnamed x7, local copies, waits for them, and re-layouts  3.29 us

profile of v3, /device:TPU:7, one launch (start us, length us, event | category | flops | bytes accessed | tf_op | source)
XLA Modules:
  0.0 67.0 jit_solution(12029345552557718424)
XLA Ops:
  0.6 63.1 %banded_backward.1 = (bf16[32,6144]{1,0:T(8,128)(2,1)}, bf16[32,1024]{1,0:T(8,128)(2,1)}, bf16[32,1024]{1,0:T(8,128)(2,1)}) custom-call(bf16[32,6144]{1,0:T(8,128)(2,1)} %q_ref.1, bf16[32,1024]{1,0:T(8,128)(2,1)} %k_ref.1, bf16[32,1024]{1,0:T(8,128)(2,1)} %v_ref.1, bf16[32,6144]{1,0:T(8,128)(2,1)} %go_ref.1, s32[1,128]{1,0:T(1,128)} %bitcast.1), custom_call_target="tpu_custom_call" | custom-call | tf_op jit(solution)/shard_map/banded_backward/pallas_call | solution.py:480
  63.7 0.0 copy-start.1
  63.7 1.8 %copy.11 = bf16[32,6144]{1,0:T(8,128)(2,1)} copy(bf16[32,6144]{1,0:T(8,128)(2,1)} %get-tuple-element.6) | data formatting | bytes 786432
  65.5 0.0 copy-done.1
  65.5 0.0 copy-start
  65.5 0.6 copy.12
  66.1 0.2 copy-done
  66.4 0.6 copy.13
Async XLA Ops:
  63.7 1.8 %copy-start.1 = (bf16[32,1024]{1,0:T(8,128)(2,1)S(1)}, bf16[32,1024]{1,0:T(8,128)(2,1)}, u32[]{:S(2)}) copy-start(bf16[32,1024]{1,0:T(8,128)(2,1)} %get-tuple-element.7) | copy-start | bytes 196612
  65.5 0.9 %copy-start = (bf16[32,1024]{1,0:T(8,128)(2,1)S(1)}, bf16[32,1024]{1,0:T(8,128)(2,1)}, u32[]{:S(2)}) copy-start(bf16[32,1024]{1,0:T(8,128)(2,1)} %get-tuple-element.8) | copy-start | bytes 196612

commit v4 on v3

--- a/solution.py
+++ b/solution.py
@@ -12,6 +12,7 @@
 NX = 4
 KVH = 8
 MESH = pl.DeviceIdType.MESH
+TILE = 256
 NEG = -1e30
 SCALE = D ** -0.5
 EXP_SCALE = SCALE * 1.4426950408889634
@@ -32,7 +33,7 @@
     ny, nzh, group,
     q_ref, k_ref, v_ref, go_ref, pos_ref,
     gq_ref, gk_ref, gv_ref,
-    kst, vst, staged, poss, kv, qbuf, gbuf, qrow, grow, q_t, g_t, pst, dpst, mst, mrun, lrun, drun, dq_t,
+    kst, vst, staged, poss, kv, qbuf, gbuf, qrow, grow, q_t, g_t, pst, mst, mrun, lrun, drun, dq_t,
     acc, part, rbuf, sib_out, sib_in, kv_out, kv_in, prior_in, gq_out,
     ls, fs, fr, os, orr, ks, hs, hr, rs, rr, ss, sr, bs, br, ps, pr, ready,
 ):
@@ -270,40 +271,43 @@
     key_off = lax.rem(lax.broadcasted_iota(jnp.int32, (128, 128), 0), RUN).astype(F32)
     row_off = lax.rem(lax.broadcasted_iota(jnp.int32, (8, 128), 1), RUN).astype(F32)
 
+    penalty = jnp.where(first, -NEG, 0.0)
+
     def rows_of(origin, qb, which):
         at = [pl.ds(hd2 * 64 + which * 32, 32) for hd2 in range(4)]
         return jnp.concatenate([kv[origin, qb + p, rows, :] for p in range(2) for rows in at], axis=0)
 
     def forward_chunk(origin):
-        def block(qb, _):
-            scores = dot(rows_of(origin, qb, 0), q_t[qb])
-            dprobs = dot(rows_of(origin, qb, 1), g_t[qb])
-            dpst[origin, qb] = dprobs
+        for qb in range(2):
+            keys, vals = rows_of(origin, qb, 0), rows_of(origin, qb, 1)
             runs = kv[origin, qb + 1, pl.ds(256, 16), :].astype(F32)[:1, :]
             key_pos = jnp.broadcast_to(runs, (128, 128)).T * RUN + key_off
             row_runs = kv[y, qb + 1, pl.ds(256, 16), :].astype(F32)[:1, :]
             allowed = key_pos <= row_runs * RUN + row_off[:1, :]
-            penalty = jnp.where(jnp.logical_and(first, qb == 0), -NEG, 0.0)
-            prior = scores[:128]
-            near = jnp.concatenate(
-                [jnp.where(allowed, scores[128:, g * D:(g + 1) * D], NEG) for g in range(group)], axis=1
-            )
-            prior_top = jnp.max(prior, axis=0, keepdims=True) - penalty
-            old = mrun[qb]
-            top = jnp.maximum(old, jnp.maximum(prior_top, jnp.max(near, axis=0, keepdims=True)))
-            mrun[qb] = top
-            mst[origin, qb] = top
-            shift = top * EXP_SCALE
-            probs = jnp.concatenate(
-                [jnp.exp2(prior * EXP_SCALE - (shift + penalty)), jnp.exp2(near * EXP_SCALE - shift)], axis=0
-            )
-            faded = jnp.exp2((old - top) * EXP_SCALE)
-            lrun[qb] = lrun[qb] * faded + sum8(probs)
-            drun[qb] = drun[qb] * faded + sum8(probs * dprobs)
-            pst[origin, qb] = probs.astype(BF16)
-            return 0
-
-        lax.fori_loop(0, 2, block, 0)
+            for tile in range(0, width, TILE):
+                cols = slice(tile, tile + TILE)
+                scores = dot(keys, q_t[qb, :, cols])
+                prior = scores[:128]
+                near = jnp.concatenate(
+                    [jnp.where(allowed, scores[128:, g:g + D], NEG) for g in range(0, TILE, D)], axis=1
+                )
+                prior_top = jnp.max(prior, axis=0, keepdims=True)
+                if qb == 0:
+                    prior_top = prior_top - penalty
+                old = mrun[qb, :, cols]
+                top = jnp.maximum(old, jnp.maximum(prior_top, jnp.max(near, axis=0, keepdims=True)))
+                mrun[qb, :, cols] = top
+                mst[origin, qb, :, cols] = top
+                shift = top * EXP_SCALE
+                prior_shift = shift + penalty if qb == 0 else shift
+                probs = jnp.concatenate(
+                    [jnp.exp2(prior * EXP_SCALE - prior_shift), jnp.exp2(near * EXP_SCALE - shift)], axis=0
+                )
+                faded = jnp.exp2((old - top) * EXP_SCALE)
+                lrun[qb, :, cols] = lrun[qb, :, cols] * faded + sum8(probs)
+                pst[origin, qb, :, cols] = probs.astype(BF16)
+                dprobs = dot(vals, g_t[qb, :, cols])
+                drun[qb, :, cols] = drun[qb, :, cols] * faded + sum8(probs * dprobs)
 
     def chunk_at(d, j):
         return lax.rem(y + ny + (1 - 2 * j) * d, ny)
@@ -329,16 +333,20 @@
     def backward_chunk(d, j):
         origin = chunk_at(d, j)
 
-        def block(qb, _):
-            weight = jnp.exp2((mst[origin, qb] - mrun[qb]) * EXP_SCALE) * lrun[qb, :1, :]
-            probs = pst[origin, qb].astype(F32) * weight
-            dscores = (probs * (dpst[origin, qb] - drun[qb, :1, :])).astype(BF16)
-            acc[origin, qb, 0] = dot(dscores, qrow[qb]) * SCALE
-            acc[origin, qb, 1] = dot(probs.astype(BF16), grow[qb])
-            dq_t[qb] += dot(rows_of(origin, qb, 0).T, dscores)
-            return 0
-
-        lax.fori_loop(0, 2, block, 0)
+        for qb in range(2):
+            keys, vals = rows_of(origin, qb, 0), rows_of(origin, qb, 1)
+            probs16, dscores16 = [], []
+            for tile in range(0, width, TILE):
+                cols = slice(tile, tile + TILE)
+                weight = jnp.exp2((mst[origin, qb, :, cols] - mrun[qb, :, cols]) * EXP_SCALE) * lrun[qb, :1, cols]
+                probs = pst[origin, qb, :, cols].astype(F32) * weight
+                dprobs = dot(vals, g_t[qb, :, cols])
+                probs16.append(probs.astype(BF16))
+                dscores16.append((probs * (dprobs - drun[qb, :1, cols])).astype(BF16))
+            dscores = jnp.concatenate(dscores16, axis=1)
+            acc[origin, qb, 1] = dot(jnp.concatenate(probs16, axis=1), grow[qb])
+            acc[origin, qb, 0] = dot(dscores, qrow[qb])
+            dq_t[qb] += dot(keys.T, dscores)
 
         @pl.when(core1)
         def _():
@@ -403,7 +411,7 @@
             for s2 in range(2):
                 for g in range(group):
                     cols = slice(g * D, (g + 1) * D)
-                    gq_out[s2, :, cols] = (dq_t[s2, :, cols].T * SCALE).astype(BF16)
+                    gq_out[s2, :, cols] = dq_t[s2, :, cols].T.astype(BF16)
             pl.semaphore_wait(ready, 8 - own.astype(jnp.int32))
             q_cols = pl.ds(pl.multiple_of(kvh * width, D), width)
             for m, (device, hd2, s2, me) in enumerate(back):
@@ -477,7 +485,7 @@
     anywhere = pl.BlockSpec(memory_space=pl.ANY)
     vmem = pl.BlockSpec(memory_space=pltpu.VMEM)
     dma = pltpu.SemaphoreType.DMA
-    return pl.pallas_call(
+    grad_query, grad_key, grad_value = pl.pallas_call(
         functools.partial(kernel, ny, nzh, group),
         out_shape=tuple(jax.ShapeDtypeStruct(a.shape, BF16) for a in (queries, keys, values)),
         in_specs=[anywhere] * 4 + [vmem],
@@ -495,7 +503,6 @@
             pltpu.VMEM((2, D, lanes), BF16),
             pltpu.VMEM((2, D, lanes), BF16),
             pltpu.VMEM((ny, 2, 256, lanes), BF16),
-            pltpu.VMEM((ny, 2, 256, lanes), F32),
             pltpu.VMEM((ny, 2, 1, lanes), F32),
             pltpu.VMEM((2, 1, lanes), F32),
             pltpu.VMEM((2, 8, lanes), F32),
@@ -526,6 +533,8 @@
         ),
         name="banded_backward",
     )(queries, keys, values, grad_out, positions.reshape(1, -1))
+    scaled = [(a.astype(F32) * SCALE).astype(BF16) for a in (grad_query, grad_key)]
+    return (*scaled, grad_value)
 
 
 def solution(mesh):

time: 67.6 us -> 65.6 us (0.970)
  other arithmetic: 0 us -> 2.48 us
  local copies, waits for them, and re-layouts: 3.29 us -> 0.83 us
  Pallas kernels: 63.1 us -> 61.4 us
    convert_element_type x0 -> x2, other arithmetic: none -> 2.48 us  [on_device(): (a.astype(F32) * SCALE).astype(BF16)]
    unnamed x7 -> x5, local copies, waits for them, and re-layouts: 3.29 us -> 0.83 us
    pallas_call x1, Pallas kernels: 63.1 us -> 61.4 us  [on_device(): pl.pallas_call(functools.partial(kernel, ny, nzh, group), out_shape=tuple...]
where the time goes in v4:
time: 65.6 us; the launch traced here: 65.4 us
  Pallas kernels  61.4 us (94%)
  other arithmetic  2.48 us (4%)
  local copies, waits for them, and re-layouts  0.83 us (1%)
    pallas_call x1, Pallas kernels, on_device(): pl.pallas_call(functools.partial(kernel, ny, nzh, group), out_shape=tuple...  61.4 us
    convert_element_type x2, other arithmetic, on_device(): (a.astype(F32) * SCALE).astype(BF16)  2.48 us

profile of v4, /device:TPU:7, one launch (start us, length us, event | category | flops | bytes accessed | tf_op | source)
XLA Modules:
  0.0 65.4 jit_solution(10660997991856436588)
XLA Ops:
  0.6 61.4 %banded_backward.1 = (bf16[32,6144]{1,0:T(8,128)(2,1)}, bf16[32,1024]{1,0:T(8,128)(2,1)}, bf16[32,1024]{1,0:T(8,128)(2,1)}) custom-call(bf16[32,6144]{1,0:T(8,128)(2,1)} %q_ref.1, bf16[32,1024]{1,0:T(8,128)(2,1)} %k_ref.1, bf16[32,1024]{1,0:T(8,128)(2,1)} %v_ref.1, bf16[32,6144]{1,0:T(8,128)(2,1)} %go_ref.1, s32[1,128]{1,0:T(1,128)} %bitcast.1), custom_call_target="tpu_custom_call" | custom-call | tf_op jit(solution)/shard_map/banded_backward/pallas_call | solution.py:488
  62.0 0.0 copy-start.1
  62.1 1.8 %multiply_convert_fusion = bf16[32,6144]{1,0:T(8,128)(2,1)} fusion(bf16[32,6144]{1,0:T(8,128)(2,1)} %get-tuple-element.6), kind=kLoop, calls=%fused_computation | loop fusion | flops 589824 | bytes 786432 | tf_op jit(solution)/shard_map/convert_element_type | solution.py:536
  63.9 0.0 copy-done.1
  63.9 0.0 copy-start
  63.9 0.6 multiply_convert_fusion.1
  64.5 0.2 copy-done
  64.7 0.6 copy.9
Async XLA Ops:
  62.0 1.9 %copy-start.1 = (bf16[32,1024]{1,0:T(8,128)(2,1)S(1)}, bf16[32,1024]{1,0:T(8,128)(2,1)}, u32[]{:S(2)}) copy-start(bf16[32,1024]{1,0:T(8,128)(2,1)} %get-tuple-element.7) | copy-start | bytes 196612
  63.9 0.8 %copy-start = (bf16[32,1024]{1,0:T(8,128)(2,1)S(1)}, bf16[32,1024]{1,0:T(8,128)(2,1)}, u32[]{:S(2)}) copy-start(bf16[32,1024]{1,0:T(8,128)(2,1)} %get-tuple-element.14) | copy-start | bytes 196612

commit v5 on v4

--- a/solution.py
+++ b/solution.py
@@ -312,17 +312,24 @@
     def chunk_at(d, j):
         return lax.rem(y + ny + (1 - 2 * j) * d, ny)
 
-    chunks = [(0, 0)] + [(d, j) for d in range(1, half - 1) for j in range(2)]
-    events = gather_events(half - 1)
-    for i, event in enumerate(events):
+    def between(events, work, jobs):
+        for i, event in enumerate(events):
+            event()
+            for job in jobs[i * len(jobs) // len(events):(i + 1) * len(jobs) // len(events)]:
+                work(*job)
+
+    def forward_at(d, j):
+        forward_chunk(chunk_at(d, j))
+
+    between(gather_events(half - 1), forward_at, [(0, 0)] + [(d, j) for d in range(1, half - 1) for j in range(2)])
+    forward_at(half - 1, 0)
+    last = gather_events(half)
+    for event in last[:2]:
         event()
-        for d, j in chunks[i * len(chunks) // len(events):(i + 1) * len(chunks) // len(events)]:
-            forward_chunk(chunk_at(d, j))
-    for j in range(2):
-        forward_chunk(chunk_at(half - 1, j))
-    for event in gather_events(half):
+    forward_at(half - 1, 1)
+    for event in last[2:]:
         event()
-    forward_chunk(chunk_at(half, 0))
+    forward_at(half, 0)
 
     for qb in range(2):
         inverse = 1.0 / jnp.sum(lrun[qb], axis=0, keepdims=True)

time: 65.6 us -> 65.3 us (level)
  no operation moved by 1% of the time
where the time goes in v5:
time: 65.3 us; the launch traced here: 64.8 us
  Pallas kernels  60.8 us (93%)
  other arithmetic  2.48 us (4%)
  local copies, waits for them, and re-layouts  0.83 us (1%)
    pallas_call x1, Pallas kernels, on_device(): pl.pallas_call(functools.partial(kernel, ny, nzh, group), out_shape=tuple...  60.8 us
    convert_element_type x2, other arithmetic, on_device(): (a.astype(F32) * SCALE).astype(BF16)  2.48 us

profile of v5, /device:TPU:7, one launch (start us, length us, event | category | flops | bytes accessed | tf_op | source)
XLA Modules:
  0.0 64.8 jit_solution(13044741488343965546)
XLA Ops:
  0.6 60.8 %banded_backward.1 = (bf16[32,6144]{1,0:T(8,128)(2,1)}, bf16[32,1024]{1,0:T(8,128)(2,1)}, bf16[32,1024]{1,0:T(8,128)(2,1)}) custom-call(bf16[32,6144]{1,0:T(8,128)(2,1)} %q_ref.1, bf16[32,1024]{1,0:T(8,128)(2,1)} %k_ref.1, bf16[32,1024]{1,0:T(8,128)(2,1)} %v_ref.1, bf16[32,6144]{1,0:T(8,128)(2,1)} %go_ref.1, s32[1,128]{1,0:T(1,128)} %bitcast.1), custom_call_target="tpu_custom_call" | custom-call | tf_op jit(solution)/shard_map/banded_backward/pallas_call | solution.py:495
  61.5 0.0 copy-start.1
  61.5 1.8 %multiply_convert_fusion = bf16[32,6144]{1,0:T(8,128)(2,1)} fusion(bf16[32,6144]{1,0:T(8,128)(2,1)} %get-tuple-element.6), kind=kLoop, calls=%fused_computation | loop fusion | flops 589824 | bytes 786432 | tf_op jit(solution)/shard_map/convert_element_type | solution.py:543
  63.3 0.0 copy-done.1
  63.3 0.0 copy-start
  63.3 0.6 multiply_convert_fusion.1
  64.0 0.2 copy-done
  64.2 0.6 copy.9
Async XLA Ops:
  61.5 1.9 %copy-start.1 = (bf16[32,1024]{1,0:T(8,128)(2,1)S(1)}, bf16[32,1024]{1,0:T(8,128)(2,1)}, u32[]{:S(2)}) copy-start(bf16[32,1024]{1,0:T(8,128)(2,1)} %get-tuple-element.7) | copy-start | bytes 196612
  63.3 0.8 %copy-start = (bf16[32,1024]{1,0:T(8,128)(2,1)S(1)}, bf16[32,1024]{1,0:T(8,128)(2,1)}, u32[]{:S(2)}) copy-start(bf16[32,1024]{1,0:T(8,128)(2,1)} %get-tuple-element.14) | copy-start | bytes 196612
